TPU v7x, 32 devices: a whole 2x2x4 slice. The times are simulated.
32 devices in a mesh: leaf: 4 (over x, core), seq: 8 (over z, y).
Axes of the slice: x: 2, y: 2, z: 4, core: 2. Of those that a mesh axis runs over, the one named last changes fastest.
Arguments:
- tokens: bfloat16 [4, 1024, 2048], P('leaf', 'seq'), may hold values from -6 to 6
- parents: int32 [4, 13], P('leaf'), may hold values from 0 to 4, as said below
- lengths: int32 [4, 13], P('leaf'), may hold values from 1 to 512, as said below
- norm_attn: float32 [2048], P('seq'), may hold values from 0.5 to 1.5
- w_query: float32 [2048, 2048], P('seq'), may hold values from -0.125 to 0.125
- w_key: float32 [2048, 256], P('seq'), may hold values from -0.125 to 0.125
- w_value: float32 [2048, 256], P('seq'), may hold values from -0.125 to 0.125
- w_out: float32 [2048, 2048], P('seq'), may hold values from -2 to 2
- norm_ffn: float32 [2048], P('seq'), may hold values from 0.5 to 1.5
- w_gate: float32 [2048, 5632], P('seq'), may hold values from -0.125 to 0.125
- w_up: float32 [2048, 5632], P('seq'), may hold values from -0.125 to 0.125
- w_down: float32 [5632, 2048], P('seq'), may hold values from -0.078125 to 0.078125
- cotangent: bfloat16 [4, 1024, 2048], P('leaf', 'seq'), may hold values from -6 to 6
Outputs:
- output: bfloat16 [4, 1024, 2048], P('leaf', 'seq')
- input_grad: float32 [4, 1024, 2048], P('leaf', 'seq')
- grad_norm_attn: float32 [2048], P('seq')
- grad_query: float32 [2048, 2048], P('seq')
- grad_key: float32 [2048, 256], P('seq')
- grad_value: float32 [2048, 256], P('seq')
- grad_out: float32 [2048, 2048], P('seq')
- grad_norm_ffn: float32 [2048], P('seq')
- grad_gate: float32 [2048, 5632], P('seq')
- grad_up: float32 [2048, 5632], P('seq')
- grad_down: float32 [5632, 2048], P('seq')
Inputs may be any that keep to these rules, and one draw needn't show every extreme that they name: In every tree segment 0 is the trunk and its own parent, segments 1 to 4 have parent 0, and segments after them are leaves whose parents are among 1 to 4, each branch the parent of 2 of them. In every tree the 13 lengths are positive and sum to 1024; segment 0 holds 512 tokens and is the longest.
All inputs are finite; a program needn't handle non-finite values.
Results may differ from a plain program's by a relative error of at most 0.022.
Values may be sent and summed in bfloat16 or wider, within the bound.
No kernel may reach another device: no remote copies, remote signals or barrier semaphores. Data moves between devices by JAX's collectives and lax.ppermute only.
A program may use at most 384 MiB of HBM per device.

v0:
```python
import jax
import jax.numpy as jnp
from jax import lax
from jax.sharding import PartitionSpec as P

HEADS = 32
KV_HEADS = 4
HEAD_DIM = 64


EPSILON = 1e-05
NEGATIVE = -1e30
THETA_BASE = 10000.0


def tree_layout(parent_row, length_row, tree_len):
    segments = parent_row.shape[0]
    seg_index = jnp.arange(segments, dtype=jnp.int32)
    parent_hot = (parent_row[:, None] == seg_index[None, :]).astype(jnp.float32)
    grand_hot = jnp.sum(parent_hot[:, :, None] * parent_hot[None, :, :], axis=1)
    identity = (seg_index[:, None] == seg_index[None, :]).astype(jnp.float32)
    ancestry = (identity + parent_hot + grand_hot > 0.5).astype(jnp.float32)
    starts = jnp.cumsum(length_row) - length_row
    before = jnp.sum((ancestry - identity) * length_row[None, :].astype(jnp.float32), axis=1)
    places = jnp.arange(tree_len, dtype=jnp.int32)
    segment = jnp.sum((places[:, None] >= starts[None, :]).astype(jnp.int32), axis=1) - 1
    seg_hot = (segment[:, None] == seg_index[None, :]).astype(jnp.float32)
    offset = places.astype(jnp.float32) - jnp.sum(
        seg_hot * starts[None, :].astype(jnp.float32), axis=1
    )
    position = offset + jnp.sum(seg_hot * before[None, :], axis=1)
    return (seg_hot, ancestry, position)


def angles(position):
    half_dim = HEAD_DIM // 2
    exponent = jnp.arange(half_dim, dtype=jnp.float32) * (2.0 / HEAD_DIM)
    inverse = jnp.power(THETA_BASE, -exponent)
    turned = position[:, None] * inverse[None, :]
    turned = jnp.concatenate([turned, turned], axis=1)
    return (jnp.cos(turned), jnp.sin(turned))


def rms_scale(values, gain):
    return values * lax.rsqrt(jnp.mean(values * values, axis=-1, keepdims=True) + EPSILON) * gain


def rotate(values, cosine, sine_table):
    half_dim = values.shape[-1] // 2
    turned = jnp.concatenate([-values[..., half_dim:], values[..., :half_dim]], axis=-1)
    return values * cosine + turned * sine_table


def unrotate(grads, cosine, sine_table):
    half_dim = grads.shape[-1] // 2
    turned = grads * sine_table
    return grads * cosine + jnp.concatenate(
        [turned[..., half_dim:], -turned[..., :half_dim]], axis=-1
    )


def on_device(
    tokens,
    parents,
    lengths,
    norm_attn,
    w_query,
    w_key,
    w_value,
    w_out,
    norm_ffn,
    w_gate,
    w_up,
    w_down,
    cotangent,
):
    tree_count, tree_rows, width = tokens.shape
    seq_count = lax.axis_size("seq")
    tree_len = tree_rows * seq_count
    local_rows = tree_count * tree_rows
    group_size = HEADS // KV_HEADS
    kv_width = KV_HEADS * HEAD_DIM
    hidden_units = w_gate.shape[1]
    score_scale = HEAD_DIM ** (-0.5)
    block_len = min(512, tree_len)
    block_count = tree_len // block_len
    f32 = jnp.float32
    bf16 = jnp.bfloat16
    seg_hot, ancestry, position = jax.vmap(
        lambda parent_row, length_row: tree_layout(parent_row, length_row, tree_len)
    )(parents, lengths)
    first_row = lax.axis_index("seq") * tree_rows
    local_hot = lax.dynamic_slice_in_dim(seg_hot, first_row, tree_rows, 1)
    local_position = lax.dynamic_slice_in_dim(position, first_row, tree_rows, 1)
    cosine, sine_table = angles(local_position.reshape(local_rows))
    query_reach = jnp.einsum("brs,bst->brt", local_hot, ancestry)
    query_place = first_row + jnp.arange(tree_rows, dtype=jnp.int32)
    key_hot = seg_hot.reshape(tree_count, block_count, block_len, -1).transpose(1, 0, 2, 3)
    key_first = jnp.arange(block_count, dtype=jnp.int32) * block_len
    gain_attn_low = norm_attn.astype(bf16)
    query_low_w = w_query.astype(bf16)
    key_low_w = w_key.astype(bf16)
    value_low_w = w_value.astype(bf16)
    out_low_w = w_out.astype(bf16)
    gain_ffn_low = norm_ffn.astype(bf16)
    gate_low_w = w_gate.astype(bf16)
    up_low_w = w_up.astype(bf16)
    down_low_w = w_down.astype(bf16)
    gain_attn, query_weight, key_weight, value_weight, out_weight = (
        lax.all_gather(gain_attn_low, "seq", axis=0, tiled=True),
        lax.all_gather(query_low_w, "seq", axis=0, tiled=True),
        lax.all_gather(key_low_w, "seq", axis=0, tiled=True),
        lax.all_gather(value_low_w, "seq", axis=0, tiled=True),
        lax.all_gather(out_low_w, "seq", axis=0, tiled=True),
    )
    inputs = tokens.reshape(local_rows, width).astype(f32)
    gain_one = gain_attn.astype(f32)
    normed_low = rms_scale(inputs, gain_one).astype(bf16)
    queries = jnp.dot(normed_low, query_weight, preferred_element_type=f32)
    key_rows = jnp.dot(normed_low, key_weight, preferred_element_type=f32)
    value_rows = jnp.dot(normed_low, value_weight, preferred_element_type=f32)
    query_low = rotate(
        queries.reshape(local_rows, HEADS, HEAD_DIM), cosine[:, None, :], sine_table[:, None, :]
    ).astype(bf16)
    key_low = rotate(
        key_rows.reshape(local_rows, KV_HEADS, HEAD_DIM), cosine[:, None, :], sine_table[:, None, :]
    ).astype(bf16)
    value_low = value_rows.astype(bf16)
    key_all, value_all = (
        lax.all_gather(key_low.reshape(tree_count, tree_rows, kv_width), "seq", axis=1, tiled=True),
        lax.all_gather(
            value_low.reshape(tree_count, tree_rows, kv_width), "seq", axis=1, tiled=True
        ),
    )
    key_blocks = key_all.reshape(tree_count, block_count, block_len, KV_HEADS, HEAD_DIM).transpose(
        1, 0, 2, 3, 4
    )
    value_blocks = value_all.reshape(
        tree_count, block_count, block_len, KV_HEADS, HEAD_DIM
    ).transpose(1, 0, 2, 3, 4)
    query_heads = query_low.reshape(tree_count, tree_rows, KV_HEADS, group_size, HEAD_DIM)
    blocks = (key_blocks, value_blocks, key_hot, key_first)
    head_shape = (tree_count, tree_rows, KV_HEADS, group_size)
    empty_out = jnp.zeros((), f32)

    def block_mask(hot_block, block_first):
        seg_reach = jnp.einsum("brs,bks->brk", query_reach, hot_block) > 0.5
        in_order = (block_first + jnp.arange(block_len, dtype=jnp.int32))[None, :] <= query_place[
            :, None
        ]
        return seg_reach & in_order[None, :, :]

    def block_scores(key_block, allowed):
        scores = (
            jnp.einsum("brgeh,bkgh->brgek", query_heads, key_block, preferred_element_type=f32)
            * score_scale
        )
        return jnp.where(allowed[:, :, None, None, :], scores, NEGATIVE)

    def peak_step(carried, block_item):
        key_block, value_block, hot_block, block_first = block_item
        allowed = block_mask(hot_block, block_first)
        row_peak, row_total = carried
        scores = block_scores(key_block, allowed)
        new_peak = jnp.maximum(row_peak, jnp.max(scores, axis=-1))
        new_total = row_total * jnp.exp(row_peak - new_peak) + jnp.sum(
            jnp.exp(scores - new_peak[..., None]), axis=-1
        )
        return ((new_peak, new_total), empty_out)

    peak_init = (jnp.full(head_shape, NEGATIVE, f32), jnp.zeros(head_shape, f32))
    (row_peak, row_total), unused_peak = lax.scan(peak_step, peak_init, blocks)
    log_total = row_peak + jnp.log(row_total)

    def out_step(carried, block_item):
        key_block, value_block, hot_block, block_first = block_item
        allowed = block_mask(hot_block, block_first)
        scores = block_scores(key_block, allowed)
        weights = jnp.exp(scores - log_total[..., None]).astype(bf16)
        return (
            carried
            + jnp.einsum("brgek,bkgh->brgeh", weights, value_block, preferred_element_type=f32),
            empty_out,
        )

    attended, unused_out = lax.scan(out_step, jnp.zeros(head_shape + (HEAD_DIM,), f32), blocks)
    attended_low = attended.reshape(local_rows, width).astype(bf16)
    hidden_state = inputs + jnp.dot(attended_low, out_weight, preferred_element_type=f32)
    gain_ffn, gate_weight, up_weight, down_weight = (
        lax.all_gather(gain_ffn_low, "seq", axis=0, tiled=True),
        lax.all_gather(gate_low_w, "seq", axis=0, tiled=True),
        lax.all_gather(up_low_w, "seq", axis=0, tiled=True),
        lax.all_gather(down_low_w, "seq", axis=0, tiled=True),
    )
    gain_two = gain_ffn.astype(f32)
    second_low = rms_scale(hidden_state, gain_two).astype(bf16)
    gate_value = jnp.dot(second_low, gate_weight, preferred_element_type=f32)
    up_value = jnp.dot(second_low, up_weight, preferred_element_type=f32)
    activated = (jax.nn.silu(gate_value) * up_value).astype(bf16)
    result = hidden_state + jnp.dot(activated, down_weight, preferred_element_type=f32)
    output = result.reshape(tree_count, tree_rows, width).astype(bf16)
    gain_ffn, gate_weight, up_weight, down_weight = (
        lax.all_gather(gain_ffn_low, "seq", axis=0, tiled=True),
        lax.all_gather(gate_low_w, "seq", axis=0, tiled=True),
        lax.all_gather(up_low_w, "seq", axis=0, tiled=True),
        lax.all_gather(down_low_w, "seq", axis=0, tiled=True),
    )
    gain_attn, query_weight, key_weight, value_weight, out_weight = (
        lax.all_gather(gain_attn_low, "seq", axis=0, tiled=True),
        lax.all_gather(query_low_w, "seq", axis=0, tiled=True),
        lax.all_gather(key_low_w, "seq", axis=0, tiled=True),
        lax.all_gather(value_low_w, "seq", axis=0, tiled=True),
        lax.all_gather(out_low_w, "seq", axis=0, tiled=True),
    )
    cot_rows = cotangent.reshape(local_rows, width).astype(f32)
    cot_low = cot_rows.astype(bf16)
    hidden_grad = jnp.einsum("td,fd->tf", cot_low, down_weight, preferred_element_type=f32)
    unused_value, gate_pull = jax.vjp(
        lambda gate_in, up_in: jax.nn.silu(gate_in) * up_in, gate_value, up_value
    )
    gate_grad, up_grad = gate_pull(hidden_grad)
    gate_up_low = jnp.concatenate([gate_grad, up_grad], axis=1).astype(bf16)
    second_grad = jnp.einsum(
        "tf,df->td", gate_up_low[:, :hidden_units], gate_weight, preferred_element_type=f32
    )
    second_grad = second_grad + jnp.einsum(
        "tf,df->td", gate_up_low[:, hidden_units:], up_weight, preferred_element_type=f32
    )
    unused_second, norm_pull = jax.vjp(rms_scale, hidden_state, gain_two)
    state_norm_grad, ffn_gain_grad = norm_pull(second_grad)
    state_grad = cot_rows + state_norm_grad
    columns = second_low
    gate_up_part = lax.psum_scatter(
        jnp.einsum("tc,tf->cf", columns, gate_up_low, preferred_element_type=f32).astype(
            jnp.bfloat16
        ),
        "seq",
        scatter_dimension=0,
        tiled=True,
    ).astype(jnp.float32)
    columns = activated
    down_part = lax.psum_scatter(
        jnp.einsum("tc,td->cd", columns, cot_low, preferred_element_type=f32).astype(jnp.bfloat16),
        "seq",
        scatter_dimension=0,
        tiled=True,
    )
    state_low = state_grad.astype(bf16)
    out_weight_grad = jnp.einsum("tc,td->cd", attended_low, state_low, preferred_element_type=f32)
    attended_grad = jnp.einsum(
        "td,cd->tc", state_low, out_weight, preferred_element_type=f32
    ).astype(bf16)
    attended_grad = attended_grad.reshape(tree_count, tree_rows, KV_HEADS, group_size, HEAD_DIM)

    def delta_step(carried, block_item):
        key_block, value_block, hot_block, block_first = block_item
        allowed = block_mask(hot_block, block_first)
        scores = block_scores(key_block, allowed)
        weights = jnp.exp(scores - log_total[..., None])
        value_dots = jnp.einsum(
            "brgeh,bkgh->brgek", attended_grad, value_block, preferred_element_type=f32
        )
        return (carried + jnp.sum(weights * value_dots, axis=-1), empty_out)

    row_delta, unused_delta = lax.scan(delta_step, jnp.zeros(head_shape, f32), blocks)

    def grad_step(carried, block_item):
        key_block, value_block, hot_block, block_first = block_item
        allowed = block_mask(hot_block, block_first)
        running = carried
        scores = block_scores(key_block, allowed)
        weights = jnp.exp(scores - log_total[..., None])
        value_dots = jnp.einsum(
            "brgeh,bkgh->brgek", attended_grad, value_block, preferred_element_type=f32
        )
        score_grad = (weights * (value_dots - row_delta[..., None])).astype(bf16)
        running = running + jnp.einsum(
            "brgek,bkgh->brgeh", score_grad, key_block, preferred_element_type=f32
        )
        key_grad = (
            jnp.einsum("brgek,brgeh->bkgh", score_grad, query_heads, preferred_element_type=f32)
            * score_scale
        )
        value_grad = jnp.einsum(
            "brgek,brgeh->bkgh", weights.astype(bf16), attended_grad, preferred_element_type=f32
        )
        joined = jnp.concatenate(
            [
                key_grad.reshape(tree_count, block_len, kv_width),
                value_grad.reshape(tree_count, block_len, kv_width),
            ],
            axis=2,
        )
        return (running, joined)

    query_grad, kv_blocks = lax.scan(grad_step, jnp.zeros(head_shape + (HEAD_DIM,), f32), blocks)
    kv_terms = kv_blocks.transpose(1, 0, 2, 3).reshape(tree_count, tree_len, 2 * kv_width)
    kv_local = lax.psum_scatter(
        kv_terms.astype(jnp.bfloat16), "seq", scatter_dimension=1, tiled=True
    ).astype(jnp.float32)
    key_rot_grad = kv_local[:, :, :kv_width].reshape(local_rows, KV_HEADS, HEAD_DIM)
    value_grad_low = kv_local[:, :, kv_width:].reshape(local_rows, kv_width).astype(bf16)
    key_grad_low = (
        unrotate(key_rot_grad, cosine[:, None, :], sine_table[:, None, :])
        .reshape(local_rows, kv_width)
        .astype(bf16)
    )
    query_rot_grad = (query_grad * score_scale).reshape(local_rows, HEADS, HEAD_DIM)
    query_grad_low = (
        unrotate(query_rot_grad, cosine[:, None, :], sine_table[:, None, :])
        .reshape(local_rows, width)
        .astype(bf16)
    )
    query_weight_grad = jnp.einsum(
        "tc,td->cd", normed_low, query_grad_low, preferred_element_type=f32
    )
    key_weight_grad = jnp.einsum("tc,td->cd", normed_low, key_grad_low, preferred_element_type=f32)
    value_weight_grad = jnp.einsum(
        "tc,td->cd", normed_low, value_grad_low, preferred_element_type=f32
    )
    normed_grad = jnp.einsum("td,cd->tc", query_grad_low, query_weight, preferred_element_type=f32)
    normed_grad = normed_grad + jnp.einsum(
        "td,cd->tc", key_grad_low, key_weight, preferred_element_type=f32
    )
    normed_grad = normed_grad + jnp.einsum(
        "td,cd->tc", value_grad_low, value_weight, preferred_element_type=f32
    )
    unused_first, first_pull = jax.vjp(rms_scale, inputs, gain_one)
    input_norm_grad, attn_gain_grad = first_pull(normed_grad)
    input_grad = (state_grad + input_norm_grad).reshape(tree_count, tree_rows, width)
    attn_part = (
        lax.psum_scatter(
            attn_gain_grad.astype(jnp.bfloat16), "seq", scatter_dimension=0, tiled=True
        ).astype(jnp.float32),
        lax.psum_scatter(
            query_weight_grad.astype(jnp.bfloat16), "seq", scatter_dimension=0, tiled=True
        ).astype(jnp.float32),
        lax.psum_scatter(
            key_weight_grad.astype(jnp.bfloat16), "seq", scatter_dimension=0, tiled=True
        ).astype(jnp.float32),
        lax.psum_scatter(
            value_weight_grad.astype(jnp.bfloat16), "seq", scatter_dimension=0, tiled=True
        ).astype(jnp.float32),
        lax.psum_scatter(
            out_weight_grad.astype(jnp.bfloat16), "seq", scatter_dimension=0, tiled=True
        ).astype(jnp.float32),
        lax.psum_scatter(
            ffn_gain_grad.astype(jnp.bfloat16), "seq", scatter_dimension=0, tiled=True
        ).astype(jnp.float32),
    )
    summed = (
        lax.psum(attn_part[0].astype(jnp.bfloat16), "leaf").astype(jnp.float32),
        lax.psum(attn_part[1].astype(jnp.bfloat16), "leaf").astype(jnp.float32),
        lax.psum(attn_part[2].astype(jnp.bfloat16), "leaf").astype(jnp.float32),
        lax.psum(attn_part[3].astype(jnp.bfloat16), "leaf").astype(jnp.float32),
        lax.psum(attn_part[4].astype(jnp.bfloat16), "leaf").astype(jnp.float32),
        lax.psum(attn_part[5].astype(jnp.bfloat16), "leaf").astype(jnp.float32),
        lax.psum(gate_up_part[:, :hidden_units].astype(jnp.bfloat16), "leaf").astype(jnp.float32),
        lax.psum(gate_up_part[:, hidden_units:].astype(jnp.bfloat16), "leaf").astype(jnp.float32),
        lax.psum(down_part, "leaf").astype(jnp.float32),
    )
    return (
        output,
        input_grad,
        summed[0],
        summed[1],
        summed[2],
        summed[3],
        summed[4],
        summed[5],
        summed[6],
        summed[7],
        summed[8],
    )


def solution(mesh):
    return jax.shard_map(
        on_device,
        mesh=mesh,
        in_specs=(
            P("leaf", "seq", None),
            P("leaf", None),
            P("leaf", None),
            P("seq"),
            P("seq", None),
            P("seq", None),
            P("seq", None),
            P("seq", None),
            P("seq"),
            P("seq", None),
            P("seq", None),
            P("seq", None),
            P("leaf", "seq", None),
        ),
        out_specs=(
            P("leaf", "seq", None),
            P("leaf", "seq", None),
            P("seq"),
            P("seq", None),
            P("seq", None),
            P("seq", None),
            P("seq", None),
            P("seq"),
            P("seq", None),
            P("seq", None),
            P("seq", None),
        ),
        check_vma=False,
    )
```

profile of v0, /device:TPU:0, one launch (start us, length us, event | category | flops | bytes accessed | tf_op | source)
XLA Modules:
  0.0 4259.4 jit_solution(7473329737403917824)
XLA Ops:
  10.6 2.7 convert_element_type.364
  13.4 2.7 convert_element_type.368
  16.2 4.5 convert_element_type.372
  20.8 4.6 convert_element_type.373
  25.4 4.8 convert_element_type.375
  30.4 22.2 all-gather.1
  53.6 16.3 all-gather.2
  72.7 32.1 all-gather
  108.7 31.2 all_gather.44
  140.4 91.5 %all-gather.15.cloned.1.call-done = bf16[2048,2048]{1,0:T(8,128)(2,1)} async-done(((bf16[256,2048]{1,0:T(8,128)(2,1)}), bf16[2048,2048]{1,0:T(8,128)(2,1)}) %all-gather.15.cloned.1.call-update) | async-done | bytes 8388624 | tf_op jit(solution)/shard_map/all_gather | solution.py:111
  231.9 12.4 copy.116
  244.3 5.8 fusion.138
  250.5 22.7 while.48
  252.0 4.6 fusion.264
  256.7 5.1 exponential_reduce_fusion.2
  263.4 4.6 fusion.264
  268.0 5.1 exponential_reduce_fusion.2
  273.2 10.7 while.49
  274.8 3.7 fusion.272
  280.0 3.7 fusion.272
  286.3 71.3 %all-gather.17.cloned.1.call-done = bf16[2048,2048]{1,0:T(8,128)(2,1)} async-done(((bf16[256,2048]{1,0:T(8,128)(2,1)}), bf16[2048,2048]{1,0:T(8,128)(2,1)}) %all-gather.17.cloned.1.call-update) | async-done | bytes 8388624 | tf_op jit(solution)/shard_map/all_gather | solution.py:114
  357.6 4.7 multiply_reduce_fusion.2
  362.5 436.3 %all-gather.19.cloned.1.call-done = bf16[2048,5632]{1,0:T(8,128)(2,1)} async-done(((bf16[256,5632]{1,0:T(8,128)(2,1)}), bf16[2048,5632]{1,0:T(8,128)(2,1)}) %all-gather.19.cloned.1.call-update) | async-done | bytes 23068688 | tf_op jit(solution)/shard_map/all_gather | solution.py:191
  798.9 12.3 fusion.190
  811.2 430.8 %all-gather.21.cloned.1.call-done = bf16[2048,5632]{1,0:T(8,128)(2,1)} async-done(((bf16[256,5632]{1,0:T(8,128)(2,1)}), bf16[2048,5632]{1,0:T(8,128)(2,1)}) %all-gather.21.cloned.1.call-update) | async-done | bytes 23068688 | tf_op jit(solution)/shard_map/all_gather | solution.py:192
  1242.0 12.3 fusion.191
  1254.3 430.9 %all-gather.23.cloned.1.call-done = bf16[5632,2048]{1,0:T(8,128)(2,1)} async-done(((bf16[704,2048]{1,0:T(8,128)(2,1)}), bf16[5632,2048]{1,0:T(8,128)(2,1)}) %all-gather.23.cloned.1.call-update) | async-done | bytes 23068688 | tf_op jit(solution)/shard_map/all_gather | solution.py:193
  1685.2 14.9 multiply_convert_fusion
  1700.1 13.4 fusion.192
  1713.4 14.1 multiply_reduce_fusion
  1730.1 6.3 convolution_convert_fusion.6
  1737.4 13.6 while.50
  1741.4 2.8 fusion.281
  1748.2 2.8 fusion.281
  1751.0 41.4 while.51
  1755.7 5.8 fusion.296
  1761.4 3.3 fusion.297
  1766.1 3.2 fusion.298
  1776.3 5.8 fusion.296
  1782.0 3.3 fusion.297
  1786.7 3.2 fusion.298
  1792.4 20.2 convolution_convert_fusion
  1812.7 43.2 %reduce-scatter.7.cloned.1.call-done = bf16[1,128,512]{2,1,0:T(8,128)(2,1)} async-done(((bf16[1,1024,512]{2,1,0:T(8,128)(2,1)}), bf16[1,128,512]{2,1,0:T(8,128)(2,1)}) %reduce-scatter.7.cloned.1.call-update) | async-done | bytes 131088 | tf_op jit(solution)/shard_map/reduce_scatter | solution.py:298
  1862.9 5.7 convolution_convert_fusion.3
  1868.7 5.6 convolution_convert_fusion.2
  1874.4 12.3 convolution_convert_fusion.1
  1888.6 1332.0 %all-reduce.9.cloned.1.call-done = bf16[2048,11264]{1,0:T(8,128)(2,1)} async-done(((bf16[2048,11264]{1,0:T(8,128)(2,1)}), bf16[2048,11264]{1,0:T(8,128)(2,1)}) %all-reduce.9.cloned.1.call-update) | async-done | bytes 46137360
  3220.6 6.7 fusion.187
  3227.3 59.5 %reduce-scatter.11.cloned.1.call-done = bf16[256,256]{1,0:T(8,128)(2,1)} async-done(((bf16[2048,256]{1,0:T(8,128)(2,1)}), bf16[256,256]{1,0:T(8,128)(2,1)}) %reduce-scatter.11.cloned.1.call-update) | async-done | bytes 131088 | tf_op jit(solution)/shard_map/reduce_scatter | solution.py:338
  3286.8 65.9 %reduce-scatter.13.cloned.1.call-done = bf16[256,256]{1,0:T(8,128)(2,1)} async-done(((bf16[2048,256]{1,0:T(8,128)(2,1)}), bf16[256,256]{1,0:T(8,128)(2,1)}) %reduce-scatter.13.cloned.1.call-update) | async-done | bytes 131088 | tf_op jit(solution)/shard_map/reduce_scatter | solution.py:341
  3352.7 152.0 %reduce-scatter.9.cloned.1.call-done = bf16[256,2048]{1,0:T(8,128)(2,1)} async-done(((bf16[2048,2048]{1,0:T(8,128)(2,1)}), bf16[256,2048]{1,0:T(8,128)(2,1)}) %reduce-scatter.9.cloned.1.call-update) | async-done | bytes 1048592 | tf_op jit(solution)/shard_map/reduce_scatter | solution.py:335
  3504.7 151.7 %reduce-scatter.15.cloned.1.call-done = bf16[256,2048]{1,0:T(8,128)(2,1)} async-done(((bf16[2048,2048]{1,0:T(8,128)(2,1)}), bf16[256,2048]{1,0:T(8,128)(2,1)}) %reduce-scatter.15.cloned.1.call-update) | async-done | bytes 1048592 | tf_op jit(solution)/shard_map/reduce_scatter | solution.py:344
  3656.3 376.9 %reduce-scatter.17.cloned.1.call-done = bf16[704,2048]{1,0:T(8,128)(2,1)} async-done(((bf16[5632,2048]{1,0:T(8,128)(2,1)}), bf16[704,2048]{1,0:T(8,128)(2,1)}) %reduce-scatter.17.cloned.1.call-update) | async-done | bytes 2883600 | tf_op jit(solution)/shard_map/reduce_scatter | solution.py:242
  4035.2 7.3 fusion.193
  4042.5 11.9 fusion.113
  4056.5 2.8 fusion.121
  4059.3 20.5 all-reduce.3
  4079.9 6.5 all-reduce.4
  4090.1 143.8 %all-reduce.11.cloned.1.call-done = (bf16[256,2048]{1,0:T(8,128)(2,1)}, bf16[256,256]{1,0:T(8,128)(2,1)}, bf16[256,256]{1,0:T(8,128)(2,1)}, bf16[256,2048]{1,0:T...) async-done(((bf16[256,2048]{1,0:T(8,128)(2,1)}, bf16[256,256]{1,0:T(8,128)(2,1)}, bf16[256,256]{1,0:T(8,128)(2,1)}, ...) | async-done | bytes 11010064 | tf_op jit(solution)/shard_map/psum | solution.py:353
  4233.9 2.9 convert_element_type.393
  4240.1 2.8 convert_element_type.401
  4242.9 3.2 convert_element_type.405
  4246.1 3.2 convert_element_type.406
  4249.3 3.3 convert_element_type.408
  (254 shorter events, 68.0 us)
Async XLA Ops:
  7.2 63.6 %all-gather.11.cloned.1.call-start = ((), (), s32[]{:S(2)}) async-start(), calls=%async_computation.6 | async-start | bytes 1179648 | tf_op jit(solution)/shard_map/all_gather | solution.py:113
  8.9 97.7 %all-gather.13.cloned.1.call-start = ((), (), s32[]{:S(2)}) async-start(), calls=%async_computation.7 | async-start | bytes 1179648 | tf_op jit(solution)/shard_map/all_gather | solution.py:112
  10.6 221.3 %all-gather.15.cloned.1.call-start = ((), (), s32[]{:S(2)}) async-start(), calls=%async_computation.8 | async-start | bytes 9437184 | tf_op jit(solution)/shard_map/all_gather | solution.py:111
  13.4 344.2 %all-gather.17.cloned.1.call-start = ((), (), s32[]{:S(2)}) async-start(), calls=%async_computation.9 | async-start | bytes 9437184 | tf_op jit(solution)/shard_map/all_gather | solution.py:114
  16.1 782.7 %all-gather.19.cloned.1.call-start = ((), (), s32[]{:S(2)}) async-start(), calls=%async_computation.10 | async-start | bytes 25952256 | tf_op jit(solution)/shard_map/all_gather | solution.py:191
  20.7 1221.2 %all-gather.21.cloned.1.call-start = ((), (), s32[]{:S(2)}) async-start(), calls=%async_computation.11 | async-start | bytes 25952256 | tf_op jit(solution)/shard_map/all_gather | solution.py:192
  25.3 5.0 copy-start.36
  25.3 27.3 copy-start.35
  25.3 27.6 copy-start.32
  25.3 28.3 copy-start.37
  25.3 45.1 %copy-start.4 = (bf16[1,128,2048]{2,1,0:T(8,128)(2,1)S(1)}, bf16[1,128,2048]{2,1,0:T(8,128)(2,1)}, u32[]{:S(2)}) copy-start(bf16[1,128,2048]{2,1,0:T(8,128)(2,1)} %param.21) | copy-start | bytes 1572868
  25.4 1659.8 %all-gather.23.cloned.1.call-start = ((), (), s32[]{:S(2)}) async-start(), calls=%async_computation.12 | async-start | bytes 25952256 | tf_op jit(solution)/shard_map/all_gather | solution.py:193
  30.2 1825.7 %reduce-scatter.7.cloned.1.call-start = ((), (), s32[]{:S(2)}) async-start(), calls=%async_computation.13 | async-start | bytes 1179648 | tf_op jit(solution)/shard_map/reduce_scatter | solution.py:298
  52.6 191.7 %copy-start.27 = (f32[8,1,256]{2,1,0:T(1,128)}, f32[8,1,256]{2,1,0:T(1,128)S(1)}, u32[]{:S(2)}) copy-start(f32[8,1,256]{2,1,0:T(1,128)S(1)} %convert_element_type.410) | copy-start | bytes 24580
  70.4 179.8 %copy-start.21 = (f32[128,64]{0,1:T(8,128)}, f32[128,64]{0,1:T(8,128)S(1)}, u32[]{:S(2)}) copy-start(f32[128,64]{0,1:T(8,128)S(1)} %get-tuple-element.734) | copy-start | bytes 98308
  70.4 179.8 %copy-start.25 = (f32[128,64]{0,1:T(8,128)}, f32[128,64]{0,1:T(8,128)S(1)}, u32[]{:S(2)}) copy-start(f32[128,64]{0,1:T(8,128)S(1)} %get-tuple-element.735) | copy-start | bytes 98308
  70.6 0.5 copy-start.33
  70.7 173.7 %copy-start.29 = (f32[128]{0:T(128)}, f32[128]{0:T(128)S(1)}, u32[]{:S(2)}) copy-start(f32[128]{0:T(128)S(1)} %fusion.176) | copy-start | bytes 1540
  250.5 22.7 copy-start.23
  283.9 1.0 copy-start.24
  286.3 76.0 %copy-start.12 = (bf16[1,128,4,8,64]{1,4,3,2,0:T(8,128)(2,1)}, bf16[1,128,4,8,64]{1,4,3,2,0:T(8,128)(2,1)S(1)}, u32[]{:S(2)}) copy-start(bf16[1,128,4,8,64]{1,4,3,2,0:T(8,128)(2,1)S(1)} %convert_element_type.366) | copy-start | bytes 1572868
  362.3 1365.2 %copy-start.6 = (f32[128,2048]{1,0:T(8,128)}, f32[128,2048]{1,0:T(8,128)S(1)}, u32[]{:S(2)}) copy-start(f32[128,2048]{1,0:T(8,128)S(1)} %get-tuple-element.738) | copy-start | bytes 3145732
  362.5 879.4 %copy-start.14 = (bf16[128,2048]{1,0:T(8,128)(2,1)}, bf16[128,2048]{1,0:T(8,128)(2,1)S(1)}, u32[]{:S(2)}) copy-start(bf16[128,2048]{1,0:T(8,128)(2,1)S(1)} %multiply_convert_fusion.2) | copy-start | bytes 1572868
  811.2 874.0 %copy-start.19 = (bf16[1,128,2048]{2,1,0:T(8,128)(2,1)S(1)}, bf16[1,128,2048]{2,1,0:T(8,128)(2,1)}, u32[]{:S(2)}) copy-start(bf16[1,128,2048]{2,1,0:T(8,128)(2,1)} %param.33) | copy-start | bytes 1572868
  1700.1 13.4 copy-start.11
  1729.1 1.0 copy-start.8
  1737.4 13.6 copy-start.3
  1752.5 3.2 copy-start.1
  1761.4 4.6 copy-start.2
  1764.8 4.5 copy-start
  1773.1 3.2 copy-start.1
  1782.0 4.6 copy-start.2
  1785.4 4.5 copy-start
  1792.4 1428.2 %all-reduce.9.cloned.1.call-start = ((), (), s32[]{:S(2)}) async-start(), calls=%async_computation.19 | async-start | bytes 92274688
  1812.6 44.2 %copy-start.26 = (f32[128,64]{0,1:T(8,128)S(1)}, f32[128,64]{0,1:T(8,128)}, u32[]{:S(2)}) copy-start(f32[128,64]{0,1:T(8,128)} %copy-done.25) | copy-start | bytes 98308
  1812.6 44.3 %copy-start.22 = (f32[128,64]{0,1:T(8,128)S(1)}, f32[128,64]{0,1:T(8,128)}, u32[]{:S(2)}) copy-start(f32[128,64]{0,1:T(8,128)} %copy-done.21) | copy-start | bytes 98308
  1812.6 44.3 %copy-start.5 = (bf16[1,128,2048]{2,1,0:T(8,128)(2,1)S(1)}, bf16[1,128,2048]{2,1,0:T(8,128)(2,1)}, u32[]{:S(2)}) copy-start(bf16[1,128,2048]{2,1,0:T(8,128)(2,1)} %param.21) | copy-start | bytes 1572868
  1812.6 44.3 %copy-start.28 = (f32[8,1,256]{2,1,0:T(1,128)S(1)}, f32[8,1,256]{2,1,0:T(1,128)}, u32[]{:S(2)}) copy-start(f32[8,1,256]{2,1,0:T(1,128)} %copy-done.27) | copy-start | bytes 24580
  1812.6 44.3 %copy-start.30 = (f32[128]{0:T(128)S(1)}, f32[128]{0:T(128)}, u32[]{:S(2)}) copy-start(f32[128]{0:T(128)} %copy-done.29) | copy-start | bytes 1540
  1812.7 1474.1 %reduce-scatter.11.cloned.1.call-start = ((), (), s32[]{:S(2)}) async-start(), calls=%async_computation.15 | async-start | bytes 1179648 | tf_op jit(solution)/shard_map/reduce_scatter | solution.py:338
  1858.6 1494.1 %reduce-scatter.13.cloned.1.call-start = ((), (), s32[]{:S(2)}) async-start(), calls=%async_computation.16 | async-start | bytes 1179648 | tf_op jit(solution)/shard_map/reduce_scatter | solution.py:341
  1861.1 1643.6 %reduce-scatter.9.cloned.1.call-start = ((), (), s32[]{:S(2)}) async-start(), calls=%async_computation.14 | async-start | bytes 9437184 | tf_op jit(solution)/shard_map/reduce_scatter | solution.py:335
  1861.5 1.4 copy-start.10
  1862.9 5.8 copy-start.9
  1862.9 5.8 copy-start.13
  1868.6 5.7 copy-start.20
  1868.6 1787.7 %reduce-scatter.15.cloned.1.call-start = ((), (), s32[]{:S(2)}) async-start(), calls=%async_computation.17 | async-start | bytes 9437184 | tf_op jit(solution)/shard_map/reduce_scatter | solution.py:344
  1874.3 2158.9 %reduce-scatter.17.cloned.1.call-start = ((), (), s32[]{:S(2)}) async-start(), calls=%async_computation.18 | async-start | bytes 25952256 | tf_op jit(solution)/shard_map/reduce_scatter | solution.py:242
  1886.7 0.7 copy-start.38
  1886.7 2347.2 %all-reduce.11.cloned.1.call-start = ((), (), s32[]{:S(2)}) async-start(), calls=%async_computation.20 | async-start | bytes 22020096 | tf_op jit(solution)/shard_map/psum | solution.py:353
  4033.2 9.3 copy-start.7
  4033.4 9.1 copy-start.15
  4042.5 16.8 copy-start.31
  4042.5 45.1 %copy-start.34 = (f32[128]{0:T(128)S(1)}, f32[128]{0:T(128)}, u32[]{:S(2)}) copy-start(f32[128]{0:T(128)} %copy-done.33) | copy-start | bytes 1540
  4233.9 9.0 copy-start.18
  4233.9 12.2 copy-start.17
  4242.9 6.4 copy-start.16
Sparse Core Ops, SparseCore 0:
  10.7 42.8 all-gather.10
  56.4 41.7 all-gather.12
  100.8 131.0 all-gather.14
  234.4 123.1 all-gather.16
  359.6 439.2 all-gather.18
  800.8 441.0 all-gather.20
  1244.1 441.0 all-gather.22
  1792.5 63.3 reduce-scatter.6
  1860.8 1359.7 all-reduce.8
  3224.2 62.5 reduce-scatter.10
  3290.2 62.4 reduce-scatter.12
  3356.6 147.9 reduce-scatter.8
  3508.3 147.9 reduce-scatter.14
  3660.6 372.6 reduce-scatter.16
  4037.2 196.6 all-reduce.10
where the time goes:
time: 4260 us
  waiting for transfers between devices  3790 us (89%)
  matrix products  216 us (5%)
  blocking collectives  129 us (3%)
  other arithmetic  69.7 us (2%)
    unnamed x16, waiting for transfers between devices  1330 us
    all_gather x1, waiting for transfers between devices, on_device(): lax.all_gather(gate_low_w, 'seq', axis=0, tiled=True)  436 us
    all_gather x1, waiting for transfers between devices, on_device(): lax.all_gather(down_low_w, 'seq', axis=0, tiled=True)  431 us
    all_gather x1, waiting for transfers between devices, on_device(): lax.all_gather(up_low_w, 'seq', axis=0, tiled=True)  431 us
    reduce_scatter x1, waiting for transfers between devices, on_device(): lax.psum_scatter(jnp.einsum('tc,td->cd', columns, cot_low, preferred_elem...  377 us
    reduce_scatter x1, waiting for transfers between devices, on_device(): lax.psum_scatter(query_weight_grad.astype(jnp.bfloat16), 'seq', scatter_d...  152 us
    reduce_scatter x1, waiting for transfers between devices, on_device(): lax.psum_scatter(out_weight_grad.astype(jnp.bfloat16), 'seq', scatter_dim...  152 us
    psum x1, waiting for transfers between devices, on_device(): lax.psum(attn_part[1].astype(jnp.bfloat16), 'leaf').astype(jnp.float32)  144 us
  transfers between devices with their start and end apart: 15, of which 13 were waited for; matrix products, arithmetic and copies ran while one was open for 5% of the time, Pallas kernels for 0%

commit v1 on v0

v1 whole, which is shorter than its diff:
```python
import functools

import jax
import jax.numpy as jnp
from jax import lax
from jax.experimental import pallas as pl
from jax.experimental.pallas import tpu as pltpu
from jax.sharding import PartitionSpec as P

HEADS = 32
KV_HEADS = 4
HEAD_DIM = 64
GROUP = HEADS // KV_HEADS
SCALE = HEAD_DIM ** (-0.5)

EPSILON = 1e-05
NEGATIVE = -1e30
THETA_BASE = 10000.0
BOTH = ("leaf", "seq")
VMEM_LIMIT = 56 * 1024 * 1024

f32 = jnp.float32
bf16 = jnp.bfloat16

NT = (((1,), (1,)), ((), ()))
NN = (((1,), (0,)), ((), ()))
TN = (((0,), (0,)), ((), ()))


def mm(left, right, dims=NN):
    return lax.dot_general(left, right, dims, preferred_element_type=f32)


def after(value, *others):
    return lax.optimization_barrier((value, *others))[0]


def tree_layout(parent_row, length_row, tree_len):
    segments = parent_row.shape[0]
    seg_index = jnp.arange(segments, dtype=jnp.int32)
    parent_hot = (parent_row[:, None] == seg_index[None, :]).astype(f32)
    grand_hot = jnp.sum(parent_hot[:, :, None] * parent_hot[None, :, :], axis=1)
    identity = (seg_index[:, None] == seg_index[None, :]).astype(f32)
    ancestry = (identity + parent_hot + grand_hot > 0.5).astype(f32)
    earlier = seg_index[None, :] < seg_index[:, None]
    starts = jnp.sum(jnp.where(earlier, length_row[None, :], 0), axis=1)
    before = jnp.sum((ancestry - identity) * length_row[None, :].astype(f32), axis=1)
    places = jnp.arange(tree_len, dtype=jnp.int32)
    segment = jnp.sum((places[:, None] >= starts[None, :]).astype(jnp.int32), axis=1) - 1
    seg_hot = (segment[:, None] == seg_index[None, :]).astype(f32)
    offset = places.astype(f32) - jnp.sum(seg_hot * starts[None, :].astype(f32), axis=1)
    position = offset + jnp.sum(seg_hot * before[None, :], axis=1)
    reach = jnp.sum(seg_hot[:, :, None] * ancestry[None, :, :], axis=1)
    return seg_hot, reach, position


def angles(position):
    half_dim = HEAD_DIM // 2
    exponent = jnp.arange(half_dim, dtype=f32) * (2.0 / HEAD_DIM)
    inverse = jnp.power(THETA_BASE, -exponent)
    turned = position[:, None] * inverse[None, :]
    return jnp.cos(turned), jnp.sin(turned)


def turn(values, forward):
    width = values.shape[-1]
    lane = lax.broadcasted_iota(jnp.int32, values.shape, 1)
    low = lane % HEAD_DIM < HEAD_DIM // 2
    ahead = pltpu.roll(values, width - HEAD_DIM // 2, 1)
    behind = pltpu.roll(values, HEAD_DIM // 2, 1)
    if forward:
        return jnp.where(low, -ahead, behind)
    return jnp.where(low, ahead, -behind)


def qkv_kernel(x_ref, gain_ref, w_ref, cos_ref, sin_ref, a_ref, q_ref, kv_ref):
    x = x_ref[...].astype(f32)
    scale = lax.rsqrt(jnp.mean(x * x, axis=-1, keepdims=True) + EPSILON)
    a = (x * scale * gain_ref[...]).astype(bf16)
    a_ref[...] = a
    rows = mm(a, w_ref[...])
    cos, sin = cos_ref[...], sin_ref[...]
    q_width = q_ref.shape[1]
    for j in range(q_width // 128):
        u = rows[:, j * 128 : (j + 1) * 128]
        q_ref[:, j * 128 : (j + 1) * 128] = (
            (u * cos + turn(u, True) * sin).astype(bf16) * jnp.array(SCALE, bf16)
        )
    u = rows[:, q_width:]
    lane = lax.broadcasted_iota(jnp.int32, u.shape, 1)
    kv_ref[...] = jnp.where(lane < HEAD_DIM, u * cos + turn(u, True) * sin, u).astype(bf16)


def project(x, gain, weight, cos, sin):
    tokens, width = x.shape
    q_width = weight.shape[1] - 2 * HEAD_DIM
    block = min(256, tokens)
    row = lambda i: (i, 0)
    whole = lambda i: (0, 0)
    return pl.pallas_call(
        qkv_kernel,
        grid=(tokens // block,),
        in_specs=[
            pl.BlockSpec((block, width), row),
            pl.BlockSpec((1, width), whole),
            pl.BlockSpec(weight.shape, whole),
            pl.BlockSpec((block, 128), row),
            pl.BlockSpec((block, 128), row),
        ],
        out_specs=[
            pl.BlockSpec((block, width), row),
            pl.BlockSpec((block, q_width), row),
            pl.BlockSpec((block, 128), row),
        ],
        out_shape=[
            jax.ShapeDtypeStruct((tokens, width), bf16),
            jax.ShapeDtypeStruct((tokens, q_width), bf16),
            jax.ShapeDtypeStruct((tokens, 128), bf16),
        ],
        compiler_params=pltpu.CompilerParams(vmem_limit_bytes=VMEM_LIMIT),
        cost_estimate=pl.CostEstimate(
            flops=2 * tokens * width * weight.shape[1],
            bytes_accessed=4 * tokens * width + 2 * weight.size,
            transcendentals=0,
        ),
    )(x, gain, weight, cos, sin)


def half_masks():
    lane = lax.broadcasted_iota(jnp.int32, (1, 128), 1)
    low = jnp.where(lane < HEAD_DIM, 1.0, 0.0).astype(bf16)
    high = jnp.where(lane < HEAD_DIM, 0.0, 1.0).astype(bf16)
    return low, high


def fill_bias(bias_ref, hot_ref, reach_ref, place_ref, first, block, keys):
    seen = mm(hot_ref[:keys, :], reach_ref[first : first + block, :], NT)
    key_place = lax.broadcasted_iota(jnp.int32, (keys, block), 0)
    allowed = (seen > 0.5) & (key_place <= place_ref[:, first : first + block])
    bias_ref[:keys, :] = jnp.where(allowed, 0.0, NEGATIVE)


def attend_kernel(
    block, q_ref, kv_ref, vk_ref, vt_ref, hot_ref, reach_ref, place_ref, o_ref, lse_ref, bias_ref
):
    tokens, q_width = q_ref.shape
    masks = half_masks()
    for t in range(tokens // block):
        first, keys = t * block, (t + 1) * 2 * block
        fill_bias(bias_ref, hot_ref, reach_ref, place_ref, first, block, keys)

        def pair(j, carry, first=first, keys=keys):
            columns = pl.ds(pl.multiple_of(j * 128, 128), 128)
            both = q_ref[first : first + block, columns]
            outs = []
            for a in range(2):
                k_ref = (kv_ref, vk_ref)[a]
                s = mm(k_ref[:keys, :], both * masks[a], NT) + bias_ref[:keys, :]
                peak = jnp.max(s, axis=0, keepdims=True)
                e = jnp.exp(s - peak)
                total = jnp.sum(e, axis=0, keepdims=True)
                outs.append(mm(vt_ref[:, :keys], e.astype(bf16)) * (1.0 / total))
                lse_ref[j, a : a + 1, first : first + block] = peak + jnp.log(total)
            o_ref[first : first + block, columns] = jnp.concatenate(outs, axis=0).T.astype(bf16)
            return carry

        lax.fori_loop(0, q_width // 128, pair, 0)


def attend(q, kv, vk, vt, hot, reach, place, block):
    tokens, q_width = q.shape
    keys = kv.shape[0]
    pairs = q_width // 128
    return pl.pallas_call(
        functools.partial(attend_kernel, block),
        out_shape=[
            jax.ShapeDtypeStruct((tokens, q_width), bf16),
            jax.ShapeDtypeStruct((pairs, 2, tokens), f32),
        ],
        scratch_shapes=[pltpu.VMEM((keys, block), f32)],
        compiler_params=pltpu.CompilerParams(vmem_limit_bytes=VMEM_LIMIT),
        cost_estimate=pl.CostEstimate(
            flops=10 * tokens * keys * q_width, bytes_accessed=4 * tokens * q_width, transcendentals=0
        ),
    )(q, kv, vk, vt, hot, reach, place)


def pull_kernel(
    block,
    q_ref,
    g_ref,
    lse_ref,
    kv_ref,
    vk_ref,
    kt_ref,
    hot_ref,
    reach_ref,
    place_ref,
    cos_ref,
    sin_ref,
    dq_ref,
    one_ref,
    two_ref,
    bias_ref,
):
    tokens, q_width = q_ref.shape
    masks = half_masks()
    one_ref[...] = jnp.zeros_like(one_ref)
    two_ref[...] = jnp.zeros_like(two_ref)
    for t in range(tokens // block):
        first, keys = t * block, (t + 1) * 2 * block
        fill_bias(bias_ref, hot_ref, reach_ref, place_ref, first, block, keys)
        cos, sin = cos_ref[first : first + block, :], sin_ref[first : first + block, :]

        def pair(j, carry, first=first, keys=keys, cos=cos, sin=sin):
            columns = pl.ds(pl.multiple_of(j * 128, 128), 128)
            q_both = q_ref[first : first + block, columns]
            g_both = g_ref[first : first + block, columns]
            outs = []
            for a in range(2):
                k_ref = (kv_ref, vk_ref)[a]
                v_ref = (vk_ref, kv_ref)[a]
                q, g = q_both * masks[a], g_both * masks[a]
                s = mm(k_ref[:keys, :], q, NT) + bias_ref[:keys, :]
                p = jnp.exp(s - lse_ref[j, a : a + 1, first : first + block])
                dp = mm(v_ref[:keys, :], g, NT)
                delta = jnp.sum(p * dp, axis=0, keepdims=True)
                ds = (p * (dp - delta)).astype(bf16)
                outs.append(mm(kt_ref[:, :keys], ds))
                k_sum, v_sum = ((one_ref, two_ref), (two_ref, one_ref))[a]
                k_sum[:keys, :] += mm(ds, q)
                v_sum[:keys, :] += mm(p.astype(bf16), g)
            dq = jnp.concatenate(outs, axis=0).T * SCALE
            dq_ref[first : first + block, columns] = (
                dq * cos + turn(dq * sin, False)
            ).astype(bf16)
            return carry

        lax.fori_loop(0, q_width // 128, pair, 0)


def pull(q, g, lse, kv, vk, kt, hot, reach, place, cos, sin, block):
    tokens, q_width = q.shape
    keys = kv.shape[0]
    return pl.pallas_call(
        functools.partial(pull_kernel, block),
        out_shape=[
            jax.ShapeDtypeStruct((tokens, q_width), bf16),
            jax.ShapeDtypeStruct((keys, 128), f32),
            jax.ShapeDtypeStruct((keys, 128), f32),
        ],
        scratch_shapes=[pltpu.VMEM((keys, block), f32)],
        compiler_params=pltpu.CompilerParams(vmem_limit_bytes=VMEM_LIMIT),
        cost_estimate=pl.CostEstimate(
            flops=24 * tokens * keys * q_width, bytes_accessed=8 * tokens * q_width, transcendentals=0
        ),
    )(q, g, lse, kv, vk, kt, hot, reach, place, cos, sin)


class Place:
    def __init__(self):
        self.leaves, self.seqs = lax.axis_size("leaf"), lax.axis_size("seq")
        self.lines = self.seqs // 2
        leaf, seq = lax.axis_index("leaf"), lax.axis_index("seq")
        self.leaf = leaf
        self.far, self.core, self.line, self.near = leaf // 2, leaf % 2, seq // 2, seq % 2
        self.core_pairs = [(i, i ^ 1) for i in range(self.leaves)]
        self.far_pairs = [(i, i ^ 2) for i in range(self.leaves)]
        self.near_pairs = [(i, i ^ 1) for i in range(self.seqs)]
        self.square = [[], []]
        for i in range(self.leaves):
            for j in range(self.seqs):
                here = i * self.seqs + j
                far, near = (i ^ 2) * self.seqs + j, i * self.seqs + (j ^ 1)
                self.square[0].append((here, near if i % 2 else far))
                self.square[1].append((here, far if i % 2 else near))

    def shift(self, value, step, only=None):
        pairs = [
            ((a * 2 + b), (a + step) * 2 + b)
            for a in range(self.lines)
            for b in range(2)
            if 0 <= a + step < self.lines and (only is None or only(a))
        ]
        return lax.ppermute(value, "seq", pairs)

    def pick(self, stack, index, axis=0):
        return lax.dynamic_index_in_dim(stack, index, axis, keepdims=False)

    def in_order(self, ups, own, downs):
        stack = jnp.stack([*ups[::-1], own, *downs])
        return lax.dynamic_slice_in_dim(stack, self.lines - 1 - self.line, self.lines, 0)

    def line_gather(self, value):
        ups, downs = [value], [value]
        for _ in range(self.lines - 1):
            ups.append(self.shift(ups[-1], 1))
            downs.append(self.shift(downs[-1], -1))
        return self.in_order(ups[1:], value, downs[1:])

    def line_sum(self, parts):
        last = self.lines - 1
        up = down = None
        for j in range(last):
            mine_up = self.pick(parts, jnp.minimum(self.line + last - j, last))
            mine_down = self.pick(parts, jnp.maximum(self.line - last + j, 0))
            if up is not None:
                mine_up = (mine_up.astype(f32) + up.astype(f32)).astype(bf16)
                mine_down = (mine_down.astype(f32) + down.astype(f32)).astype(bf16)
            up = self.shift(mine_up, 1, lambda a, j=j: a <= j)
            down = self.shift(mine_down, -1, lambda a, j=j: a >= last - j)
        own = self.pick(parts, self.line).astype(f32)
        return own + up.astype(f32) + down.astype(f32)

    def line_swap(self, parts):
        ups, downs = [], []
        last = self.lines - 1
        for d in range(1, self.lines):
            ups.append(self.shift(self.pick(parts, jnp.minimum(self.line + d, last)), d))
            downs.append(self.shift(self.pick(parts, jnp.maximum(self.line - d, 0)), -d))
        return self.in_order(ups, self.pick(parts, self.line), downs)

    def square_gather(self, piece, axis):
        first = lax.ppermute(piece, BOTH, self.square[0])
        two = jnp.stack([piece, first])
        second = lax.ppermute(two, BOTH, self.square[1])
        four = jnp.concatenate([two, second])
        other = lax.ppermute(four, "leaf", self.core_pairs)
        pieces = []
        for near in range(2):
            for far in range(2):
                to_near, to_far = near ^ self.near, far ^ self.far
                for core in range(2):
                    index = (to_near * 2 + to_far) if core == 0 else (to_far * 2 + to_near)
                    pieces.append(
                        jnp.where(
                            self.core == core, self.pick(four, index), self.pick(other, index)
                        )
                    )
        return jnp.stack(pieces, axis)

    def square_sum(self, parts, axis):
        shape = parts.shape
        split = parts.reshape(shape[:axis] + (4, 2) + shape[axis + 1 :])
        give = self.pick(split, 1 - self.core, axis + 1)
        keep = self.pick(split, self.core, axis + 1)
        got = lax.ppermute(give, "leaf", self.core_pairs)
        four = (keep.astype(f32) + got.astype(f32)).astype(bf16)
        four = four.reshape(shape[:axis] + (2, 2) + shape[axis + 1 :])

        def side(near, far):
            return jnp.where(
                self.core == 0, self.pick(four, near, axis), self.pick(four, far, axis + 1)
            )

        got = lax.ppermute(side(1 - self.near, 1 - self.far), BOTH, self.square[1])
        two = (side(self.near, self.far).astype(f32) + got.astype(f32)).astype(bf16)
        rest = jnp.where(self.core == 0, self.far, self.near)
        got = lax.ppermute(self.pick(two, 1 - rest, axis), BOTH, self.square[0])
        return (self.pick(two, rest, axis).astype(f32) + got.astype(f32)).astype(bf16)

    def leaf_gather(self, value):
        far = lax.ppermute(value, "leaf", self.far_pairs)
        two = jnp.where(
            self.far == 0, jnp.stack([value, far]), jnp.stack([far, value])
        )
        other = lax.ppermute(two, "leaf", self.core_pairs)
        pair = jnp.where(
            self.core == 0, jnp.stack([two, other], 1), jnp.stack([other, two], 1)
        )
        return pair.reshape((4,) + value.shape)

    def sum_all(self, value):
        for axis, pairs in (
            ("leaf", self.core_pairs),
            ("leaf", self.far_pairs),
            ("seq", self.near_pairs),
        ):
            value = value + lax.ppermute(value, axis, pairs)
        return jnp.sum(self.line_gather(value), axis=0)


def rms_back(values, gain, grad):
    scale = lax.rsqrt(jnp.mean(values * values, axis=-1, keepdims=True) + EPSILON)
    inner = grad * gain
    mean = jnp.mean(inner * values, axis=-1, keepdims=True)
    return scale * inner - values * (scale * scale * scale * mean)


def on_device(
    tokens,
    parents,
    lengths,
    norm_attn,
    w_query,
    w_key,
    w_value,
    w_out,
    norm_ffn,
    w_gate,
    w_up,
    w_down,
    cotangent,
):
    at = Place()
    lines = at.lines
    _, block, width = tokens.shape
    tree_len = block * at.seqs
    rows = w_query.shape[0]
    quarter = rows // 4
    hidden = w_gate.shape[1] // lines
    heads = HEADS // lines
    q_width = heads * HEAD_DIM
    own_tokens = lines * block
    kv_of = [(i * heads) // GROUP for i in range(lines)]

    x_home = tokens[0]
    dy_home = cotangent[0]

    def quarter_of(weight):
        return lax.dynamic_slice_in_dim(weight, at.leaf * (weight.shape[0] // 4), weight.shape[0] // 4, 0)

    def columns(weight, size):
        return quarter_of(weight).astype(bf16).reshape(-1, lines, size).transpose(1, 0, 2)

    def kv_columns(weight):
        low = quarter_of(weight).astype(bf16)
        return jnp.stack([low[:, i * HEAD_DIM : (i + 1) * HEAD_DIM] for i in kv_of])

    x_all = at.line_gather(x_home)
    gains_low = jnp.stack([norm_attn.astype(bf16), norm_ffn.astype(bf16)])
    gains_near = lax.ppermute(gains_low, "seq", at.near_pairs)
    gains_two = jnp.where(
        at.near == 0, jnp.stack([gains_low, gains_near], 1), jnp.stack([gains_near, gains_low], 1)
    )
    gains = at.line_gather(gains_two).transpose(1, 0, 2, 3).reshape(2, width).astype(f32)
    gain_one, gain_two = gains[0:1], gains[1:2]

    qkv_parts = jnp.concatenate(
        [columns(w_query, q_width), kv_columns(w_key), kv_columns(w_value)], axis=2
    )
    qkv_weight = at.square_gather(at.line_swap(qkv_parts), 1).reshape(width, -1)

    seg_hot, reach, position = tree_layout(parents[0], lengths[0], tree_len)
    pad = 128 - seg_hot.shape[1]
    hot_low = jnp.pad(seg_hot, ((0, 0), (0, pad))).astype(bf16)
    spread = lambda a: at.pick(a.reshape((lines, 2, block) + a.shape[1:]), at.near, 1).reshape(
        (own_tokens,) + a.shape[1:]
    )
    reach_own = spread(jnp.pad(reach, ((0, 0), (0, pad))).astype(bf16))
    place_own = spread(jnp.arange(tree_len, dtype=jnp.int32))[None, :]
    cos, sin = angles(spread(position))
    cos, sin = jnp.tile(cos, (1, 4)), jnp.tile(sin, (1, 4))

    x_rows = x_all.reshape(own_tokens, width)
    a_one, q, kv_own = project(x_rows, gain_one, qkv_weight, cos, sin)
    kv_near = lax.ppermute(kv_own, "seq", at.near_pairs)
    own_kv, near_kv = kv_own.reshape(lines, block, 128), kv_near.reshape(lines, block, 128)
    kv = jnp.where(
        at.near == 0, jnp.stack([own_kv, near_kv], 1), jnp.stack([near_kv, own_kv], 1)
    ).reshape(tree_len, 128)
    vk = jnp.concatenate([kv[:, HEAD_DIM:], kv[:, :HEAD_DIM]], axis=1)
    kv_t = kv.T
    attended, lse = attend(q, kv, vk, kv_t[HEAD_DIM:], hot_low, reach_own, place_own, block)

    out_weight = at.square_gather(quarter_of(w_out).astype(bf16), 0).reshape(q_width, width)
    gate_up_parts = jnp.concatenate([columns(w_gate, hidden), columns(w_up, hidden)], axis=2)
    gate_up_parts = after(gate_up_parts, x_all)
    gate_up_weight = at.square_gather(at.line_swap(gate_up_parts), 1).reshape(width, 2 * hidden)
    down_weight = at.square_gather(quarter_of(w_down).astype(bf16), 0).reshape(hidden, width)

    out_parts = mm(attended, out_weight).astype(bf16).reshape(lines, block, width)
    state = x_home.astype(f32) + at.line_sum(out_parts)
    state_scale = lax.rsqrt(jnp.mean(state * state, axis=-1, keepdims=True) + EPSILON)
    second_home = (state * state_scale * gain_two).astype(bf16)
    second = at.line_gather(second_home).reshape(own_tokens, width)
    dy_home = after(dy_home, second_home)
    dy = at.line_gather(dy_home).reshape(own_tokens, width)

    gate_up = mm(second, gate_up_weight)
    gate, up = gate_up[:, :hidden], gate_up[:, hidden:]
    sigmoid = jax.nn.sigmoid(gate)
    silu = gate * sigmoid
    activated = (silu * up).astype(bf16)
    down_parts = mm(activated, down_weight).astype(bf16).reshape(lines, block, width)
    d_act = mm(dy, down_weight, NT)
    d_gate = (d_act * up * (sigmoid * (1.0 + gate * (1.0 - sigmoid)))).astype(bf16)
    d_up = (d_act * silu).astype(bf16)
    d_gate_up = jnp.concatenate([d_gate, d_up], axis=1)
    second_parts = mm(d_gate_up, gate_up_weight, NT).astype(bf16).reshape(lines, block, width)
    d_second = at.line_sum(second_parts)
    state_grad = dy_home.astype(f32) + rms_back(state, gain_two, d_second)
    gain_two_terms = jnp.sum(d_second * state * state_scale, axis=0)
    state_low = state_grad.astype(bf16)
    state_all = at.line_gather(state_low).reshape(own_tokens, width)

    down_parts = after(down_parts, state_all)
    output = (state + at.line_sum(down_parts)).astype(bf16)

    gate_up_grad = mm(second, d_gate_up, TN).astype(bf16)
    down_grad = mm(activated, dy, TN).astype(bf16)

    d_att = mm(state_all, out_weight, NT).astype(bf16)
    out_grad = mm(attended, state_all, TN).astype(bf16)
    dq, one, two = pull(
        q, d_att, lse, kv, vk, kv_t[:HEAD_DIM], hot_low, reach_own, place_own, cos, sin, block
    )
    d_kv = jnp.concatenate(
        [one[:, :HEAD_DIM] + two[:, HEAD_DIM:], one[:, HEAD_DIM:] + two[:, :HEAD_DIM]], axis=1
    ).reshape(lines, 2, block, 128)
    kv_got = lax.ppermute(at.pick(d_kv, 1 - at.near, 1).astype(bf16), "seq", at.near_pairs)
    d_kv = (at.pick(d_kv, at.near, 1) + kv_got.astype(f32)).reshape(own_tokens, 128)
    d_k, d_v = d_kv[:, :HEAD_DIM], d_kv[:, HEAD_DIM:]
    half = HEAD_DIM // 2
    turned = d_k * sin[:, :HEAD_DIM]
    d_k = d_k * cos[:, :HEAD_DIM] + jnp.concatenate([turned[:, half:], -turned[:, :half]], axis=1)
    d_qkv = jnp.concatenate([dq, d_k.astype(bf16), d_v.astype(bf16)], axis=1)
    first_wide = mm(d_qkv, qkv_weight, NT)
    x_wide = x_rows.astype(f32)
    x_scale = lax.rsqrt(jnp.mean(x_wide * x_wide, axis=-1, keepdims=True) + EPSILON)
    gain_one_terms = jnp.sum(first_wide * x_wide * x_scale, axis=0)
    d_first = at.line_sum(first_wide.astype(bf16).reshape(lines, block, width))
    input_grad = state_grad + rms_back(x_home.astype(f32), gain_one, d_first)
    qkv_grad = mm(a_one, d_qkv, TN).astype(bf16)

    def rows_home(grad):
        mine = at.square_sum(grad.reshape(8, -1, grad.shape[1]), 0)
        return at.leaf_gather(mine).reshape(-1, grad.shape[1])

    def columns_home(grad):
        mine = at.square_sum(grad.reshape(lines, 8, quarter, grad.shape[1]), 1)
        mine = at.line_swap(mine)
        return at.leaf_gather(mine.transpose(1, 0, 2)).reshape(rows, lines, grad.shape[1])

    grad_down = rows_home(down_grad).astype(f32)
    gate_up_home = columns_home(gate_up_grad)
    grad_gate = gate_up_home[:, :, :hidden].reshape(rows, -1).astype(f32)
    grad_up = gate_up_home[:, :, hidden:].reshape(rows, -1).astype(f32)
    grad_out = rows_home(out_grad).astype(f32)
    qkv_home = columns_home(qkv_grad)
    grad_query = qkv_home[:, :, :q_width].reshape(rows, -1).astype(f32)

    def kv_home(part):
        terms = [[] for _ in range(KV_HEADS)]
        for i in range(lines):
            terms[kv_of[i]].append(part[:, i, :].astype(f32))
        return jnp.concatenate([functools.reduce(jnp.add, t) for t in terms], axis=1)

    grad_key = kv_home(qkv_home[:, :, q_width : q_width + HEAD_DIM])
    grad_value = kv_home(qkv_home[:, :, q_width + HEAD_DIM :])
    gain_sums = at.sum_all(jnp.stack([gain_one_terms, gain_two_terms]))
    gain_grads = lax.dynamic_slice_in_dim(
        gain_sums, lax.axis_index("seq") * rows, rows, 1
    )
    return (
        output[None],
        input_grad[None],
        gain_grads[0],
        grad_query,
        grad_key,
        grad_value,
        grad_out,
        gain_grads[1],
        grad_gate,
        grad_up,
        grad_down,
    )


def solution(mesh):
    return jax.shard_map(
        on_device,
        mesh=mesh,
        in_specs=(
            P("leaf", "seq", None),
            P("leaf", None),
            P("leaf", None),
            P("seq"),
            P("seq", None),
            P("seq", None),
            P("seq", None),
            P("seq", None),
            P("seq"),
            P("seq", None),
            P("seq", None),
            P("seq", None),
            P("leaf", "seq", None),
        ),
        out_specs=(
            P("leaf", "seq", None),
            P("leaf", "seq", None),
            P("seq"),
            P("seq", None),
            P("seq", None),
            P("seq", None),
            P("seq", None),
            P("seq"),
            P("seq", None),
            P("seq", None),
            P("seq", None),
        ),
        check_vma=False,
    )
```

time: 4260 us -> 936 us (0.22)
  waiting for transfers between devices: 3790 us -> 335 us
  starting transfers between devices: 1.09 us -> 264 us
  matrix products: 216 us -> 51.7 us
  blocking collectives: 129 us -> 0 us
  local copies, waits for them, and re-layouts: 41.5 us -> 108 us
  other arithmetic: 69.7 us -> 122 us
    all_gather x7 -> x0, waiting for transfers between devices: 1460 us -> none  [the longest x1 436 us: on_device(): lax.all_gather(gate_low_w, 'seq', axis=0, tiled=True)]
    unnamed x16 -> x0, waiting for transfers between devices: 1330 us -> none
    reduce_scatter x6 -> x0, waiting for transfers between devices: 849 us -> none  [the longest x1 377 us: on_device(): lax.psum_scatter(jnp.einsum('tc,td->cd', columns, cot_low, preferred_elem...]
    ppermute x0 -> x122, waiting for transfers between devices: none -> 335 us  [the longest x84 246 us: shift(): return lax.ppermute(value, 'seq', pairs)]
    ppermute x0 -> x122, starting transfers between devices: none -> 264 us  [the longest x84 212 us: shift(): return lax.ppermute(value, 'seq', pairs)]
    dot_general x47 -> x11, matrix products: 216 us -> 51.7 us  [mm(): return lax.dot_general(left, right, dims, preferred_element_type=f32)]
    psum x1 -> x0, waiting for transfers between devices: 144 us -> none  [on_device(): lax.psum(attn_part[1].astype(jnp.bfloat16), 'leaf').astype(jnp.float32)]
    all_gather x4 -> x0, blocking collectives: 102 us -> none  [the longest x1 32.1 us: on_device(): lax.all_gather(value_low.reshape(tree_count, tree_rows, kv_width), 'seq',...]
  transfers between devices with their start and end apart: 15 -> 122, of which waited for: 13 -> 48; matrix products, arithmetic and copies ran while one was open for 5% -> 22% of each run, Pallas kernels for 0% -> 5%
where the time goes in v1:
time: 936 us; the launch traced here: 927 us
  waiting for transfers between devices  335 us (36%)
  starting transfers between devices  264 us (28%)
  other arithmetic  122 us (13%)
  local copies, waits for them, and re-layouts  108 us (12%)
  matrix products  51.7 us (6%)
  Pallas kernels  41.9 us (4%)
    ppermute x84, waiting for transfers between devices, shift(): return lax.ppermute(value, 'seq', pairs)  246 us
    ppermute x84, starting transfers between devices, shift(): return lax.ppermute(value, 'seq', pairs)  212 us
    dot_general x11, matrix products, mm(): return lax.dot_general(left, right, dims, preferred_element_type=f32)  51.7 us
    ppermute x4, waiting for transfers between devices, square_sum(): got = lax.ppermute(self.pick(two, 1 - rest, axis), BOTH, self.square[0])  35.4 us
    unnamed x165, local copies, waits for them, and re-layouts  28.2 us
    ppermute x4, starting transfers between devices, leaf_gather(): other = lax.ppermute(two, 'leaf', self.core_pairs)  21.3 us
    ppermute x4, waiting for transfers between devices, leaf_gather(): far = lax.ppermute(value, 'leaf', self.far_pairs)  20.3 us
    pallas_call x1, Pallas kernels, pull(): pl.pallas_call(functools.partial(pull_kernel, block), out_shape=[jax.Shap...  20.1 us
  transfers between devices with their start and end apart: 122, of which 48 were waited for; matrix products, arithmetic and copies ran while one was open for 22% of the time, Pallas kernels for 5%

profile of v1, /device:TPU:0, one launch (start us, length us, event | category | flops | bytes accessed | tf_op | source)
XLA Modules:
  0.0 926.7 jit_solution(228229245375075355)
XLA Ops:
  0.7 5.9 collective-permute-start
  14.3 6.4 collective-permute-start.13
  71.7 5.0 collective-permute-done.16
  78.0 6.8 collective-permute-done.17
  86.2 7.7 collective-permute-done.18
  96.8 4.6 collective-permute-start.1
  122.4 8.6 collective-permute-done.5
  137.0 5.9 shard_map.212
  152.1 16.0 %shard_map.213 = (bf16[512,512]{1,0:T(8,128)(2,1)}, f32[4,2,512]{2,1,0:T(2,128)}) custom-call(bf16[512,512]{1,0:T(8,128)(2,1)} %get-tuple-element.22.q_ref, bf16[1024,128]{1,0:T(8,128)(2,1)} %copy.183.kv_ref, bf16[1024,128]{1,0:T(8,128)(2,1)} %copy.184.vk_ref, bf16[64,1024]{1,0:T(8,128)(2,1)} %get-tuple-element.165.vt_ref, bf16[1024,128]{1,0:T(8,128)(2,1)} %pad.9.hot_ref, ...), custom_call_target="tpu_custom_call" | custom-call | flops 2684354560 | bytes 1048576 | tf_op jit(solution)/shard_map/pallas_call | solution.py:174
  184.9 4.9 collective-permute-start.27
  190.4 6.0 constant_dynamic-slice_fusion.7
  208.7 6.4 collective-permute-done.39
  223.6 24.8 %collective-permute-done.42 = bf16[64,2816]{1,0:T(8,128)(2,1)S(1)} collective-permute-done((bf16[64,2816]{1,0:T(8,128)(2,1)S(1)}, bf16[64,2816]{1,0:T(8,128)(2,1)S(1)}, u32[]{:S(2)}, u32[]{:S(2)}) %collective-permute-start.42) | collective-permute-done | bytes 360480 | tf_op jit(solution)/shard_map/ppermute | solution.py:285
  251.3 14.4 %stack.585 = bf16[7,64,2816]{2,0,1:T(8,128)(2,1)} concatenate(bf16[1,64,2816]{2,0,1:T(2,128)(2,1)S(1)} %copy.185, bf16[1,64,2816]{2,0,1:T(2,128)(2,1)S(1)} %copy.186, bf16[1,64,2816]{2,0,1:T(2,128)(2,1)S(1)} %copy.187, bf16[1,64,2816]{2,0,1:T(2,128)(2,1)} %get-tuple-element.127, bf16[1,64,2816]{2,0,1:T(2,128)(2,1)S(1)} %copy.188, bf16[1,64,2816]{2,0,1:T(2,128)(2,1)} %copy.189, ...), dimensions={0} | concatenate | bytes 5046272 | tf_op jit(solution)/shard_map/stack | solution.py:291
  284.2 14.7 %collective-permute-done.44 = bf16[4,64,2816]{2,0,1:T(4,128)(2,1)S(1)} collective-permute-done((bf16[4,64,2816]{2,0,1:T(4,128)(2,1)S(1)}, bf16[4,64,2816]{2,0,1:T(4,128)(2,1)S(1)}, u32[]{:S(2)}, u32[]{:S(2)}) %collective-permute-start.44) | collective-permute-done | bytes 1441824 | tf_op jit(solution)/shard_map/ppermute | solution.py:324
  302.7 4.8 collective-permute-start.32
  313.4 5.2 collective-permute-start.51
  328.6 7.0 collective-permute-done.53
  336.9 4.6 collective-permute-start.52
  351.3 4.7 collective-permute-done.54
  357.5 4.8 pad_maximum_fusion
  382.3 7.9 fusion.69
  390.3 9.3 %multiply_convert_fusion.1 = (bf16[512,1408]{1,0:T(8,128)(2,1)S(1)}, bf16[512,1408]{1,0:T(8,128)(2,1)S(1)}, bf16[512,1408]{1,0:T(8,128)(2,1)}) fusion(f32[512,2816]{1,0:T(8,128)} %fusion.69, bf16[512,2048]{1,0:T(8,128)(2,1)S(1)} %bitcast.645, bf16[1408,2048]{1,0:T(8,128)(2,1)} %bitcast.697), kind=kOutput, calls=%fused_computation.33 | convolution fusion | flops 2963603456 | bytes 17956864 | tf_op jit(solution)/shard_map/dot_general | solution.py:31
  399.5 6.4 convolution_convert_fusion.4
  406.1 4.6 collective-permute-start.56
  411.4 10.7 %collective-permute-done.56 = bf16[128,2048]{1,0:T(8,128)(2,1)S(1)} collective-permute-done((bf16[128,2048]{1,0:T(8,128)(2,1)S(1)}, bf16[128,2048]{1,0:T(8,128)(2,1)S(1)}, u32[]{:S(2)}, u32[]{:S(2)}) %collective-permute-start.56) | collective-permute-done | bytes 524320 | tf_op jit(solution)/shard_map/ppermute | solution.py:285
  422.2 4.4 collective-permute-start.57
  426.7 10.6 %collective-permute-done.57 = bf16[128,2048]{1,0:T(8,128)(2,1)S(1)} collective-permute-done((bf16[128,2048]{1,0:T(8,128)(2,1)S(1)}, bf16[128,2048]{1,0:T(8,128)(2,1)S(1)}, u32[]{:S(2)}, u32[]{:S(2)}) %collective-permute-start.57) | collective-permute-done | bytes 524320 | tf_op jit(solution)/shard_map/ppermute | solution.py:285
  438.5 5.0 collective-permute-start.58
  446.0 5.2 convolution_convert_fusion.1
  454.1 12.8 %collective-permute-done.61 = bf16[128,2048]{1,0:T(8,128)(2,1)S(1)} collective-permute-done((bf16[128,2048]{1,0:T(8,128)(2,1)S(1)}, bf16[128,2048]{1,0:T(8,128)(2,1)S(1)}, u32[]{:S(2)}, u32[]{:S(2)}) %collective-permute-start.61) | collective-permute-done | bytes 524320 | tf_op jit(solution)/shard_map/ppermute | solution.py:285
  471.7 6.9 convolution_convert_fusion
  486.0 4.6 collective-permute-start.63
  490.6 6.4 convolution_convert_fusion.6
  502.3 4.6 collective-permute-start.64
  511.0 5.4 collective-permute-done.66
  518.0 13.0 %collective-permute-done.67 = bf16[128,2048]{1,0:T(8,128)(2,1)S(1)} collective-permute-done((bf16[128,2048]{1,0:T(8,128)(2,1)S(1)}, bf16[128,2048]{1,0:T(8,128)(2,1)S(1)}, u32[]{:S(2)}, u32[]{:S(2)}) %collective-permute-start.67) | collective-permute-done | bytes 524320 | tf_op jit(solution)/shard_map/ppermute | solution.py:285
  533.4 20.1 %shard_map.214 = (bf16[512,512]{1,0:T(8,128)(2,1)}, f32[1024,128]{1,0:T(8,128)}, f32[1024,128]{1,0:T(8,128)}) custom-call(bf16[512,512]{1,0:T(8,128)(2,1)} %get-tuple-element.22.q_ref, bf16[512,512]{1,0:T(8,128)(2,1)} %convolution_convert_fusion.7.g_ref, f32[4,2,512]{2,1,0:T(2,128)} %get-tuple-element.28.lse_ref, bf16[1024,128]{1,0:T(8,128)(2,1)} %copy.183.kv_ref, ...), custom_call_target="tpu_custom_call" | custom-call | flops 6442450944 | bytes 2097152 | tf_op jit(solution)/shard_map/pallas_call | solution.py:245
  571.6 6.6 collective-permute-done.83
  584.2 4.5 collective-permute-start.85
  591.3 4.5 collective-permute-start.86
  611.3 6.3 collective-permute-done.75
  624.1 8.9 collective-permute-done.69
  642.3 5.2 collective-permute-done.76
  647.5 5.2 collective-permute-start.70
  661.7 6.0 fusion
  675.7 20.2 %collective-permute-done.103 = bf16[64,2048]{1,0:T(8,128)(2,1)S(1)} collective-permute-done((bf16[64,2048]{1,0:T(8,128)(2,1)S(1)}, bf16[64,2048]{1,0:T(8,128)(2,1)S(1)}, u32[]{:S(2)}, u32[]{:S(2)}) %collective-permute-start.103) | collective-permute-done | bytes 262176 | tf_op jit(solution)/shard_map/ppermute | solution.py:359
  699.8 7.2 collective-permute-done.73
  709.3 16.2 %collective-permute-start.121 = (bf16[2,176,2048]{2,1,0:T(8,128)(2,1)S(1)}, bf16[2,176,2048]{2,1,0:T(8,128)(2,1)S(1)}, u32[]{:S(2)}, u32[]{:S(2)}) collective-permute-start(bf16[2,176,2048]{2,1,0:T(8,128)(2,1)S(1)} %maximum_select_fusion.5), channel_id=1, source_target_pairs={{0,8},{8,0},{16,24},{24,16},{1,9},{9,1},{17,25},{25,17},{2,10},{10... | collective-permute-start | bytes 4325384 | tf_op jit(solution)/shard_map/ppermute | solution.py:367
  730.2 4.5 collective-permute-start.105
  736.2 15.1 %collective-permute-done.92 = bf16[4,64,640]{2,1,0:T(8,128)(2,1)S(1)} collective-permute-done((bf16[4,64,640]{2,1,0:T(8,128)(2,1)S(1)}, bf16[4,64,640]{2,1,0:T(8,128)(2,1)S(1)}, u32[]{:S(2)}, u32[]{:S(2)}) %collective-permute-start.92) | collective-permute-done | bytes 327712 | tf_op jit(solution)/shard_map/ppermute | solution.py:359
  760.9 5.1 collective-permute-done.109
  767.3 8.9 collective-permute-done.110
  776.3 12.8 %collective-permute-start.111 = (bf16[64,2816]{1,0:T(8,128)(2,1)S(1)}, bf16[64,2816]{1,0:T(8,128)(2,1)S(1)}, u32[]{:S(2)}, u32[]{:S(2)}) collective-permute-start(bf16[64,2816]{1,0:T(8,128)(2,1)S(1)} %get-tuple-element.121), channel_id=1, source_target_pairs={{0,2},{1,3},{2,4},{3,5},{4,6},{5,7},{8,10},{9,11},{10,12},{11,13},... | collective-permute-start | bytes 1081352 | tf_op jit(solution)/shard_map/ppermute | solution.py:285
  789.1 7.8 collective-permute-done.111
  801.3 9.0 collective-permute-done.112
  811.6 24.8 %collective-permute-done.113 = bf16[64,2816]{1,0:T(8,128)(2,1)S(1)} collective-permute-done((bf16[64,2816]{1,0:T(8,128)(2,1)S(1)}, bf16[64,2816]{1,0:T(8,128)(2,1)S(1)}, u32[]{:S(2)}, u32[]{:S(2)}) %collective-permute-start.113) | collective-permute-done | bytes 360480 | tf_op jit(solution)/shard_map/ppermute | solution.py:285
  845.6 4.6 collective-permute-done.97
  852.8 20.2 %collective-permute-done.115 = bf16[64,4,2816]{2,0,1:T(8,128)(2,1)S(1)} collective-permute-done((bf16[64,4,2816]{2,0,1:T(8,128)(2,1)S(1)}, bf16[64,4,2816]{2,0,1:T(8,128)(2,1)S(1)}, u32[]{:S(2)}, u32[]{:S(2)}) %collective-permute-start.115) | collective-permute-done | bytes 1441824 | tf_op jit(solution)/shard_map/ppermute | solution.py:363
  895.9 5.2 slice_convert_fusion
  901.2 6.3 copy.212
  907.4 6.2 copy.215
  913.7 6.3 copy.213
  919.9 6.4 copy.216
  (590 shorter events, 381.0 us)
Async XLA Ops:
  0.7 96.1 %collective-permute-start = (bf16[128,2048]{1,0:T(8,128)(2,1)}, bf16[128,2048]{1,0:T(8,128)(2,1)}, u32[]{:S(2)}, u32[]{:S(2)}) collective-permute-start(bf16[128,2048]{1,0:T(8,128)(2,1)} %bitcast.599), channel_id=1, source_target_pairs={{0,2},{1,3},{2,4},{3,5},{4,6},{5,7},{8,10},{9,11},{10,12},{11,13},... | collective-permute-start | bytes 1572872 | tf_op jit(solution)/shard_map/ppermute | solution.py:285
  6.5 100.3 %collective-permute-start.3 = (bf16[128,2048]{1,0:T(8,128)(2,1)}, bf16[128,2048]{1,0:T(8,128)(2,1)S(1)}, u32[]{:S(2)}, u32[]{:S(2)}) collective-permute-start(bf16[128,2048]{1,0:T(8,128)(2,1)} %bitcast.600), channel_id=1, source_target_pairs={{2,0},{3,1},{4,2},{5,3},{6,4},{7,5},{10,8},{11,9},{12,10},{13,11},... | collective-permute-start | bytes 1572872 | tf_op jit(solution)/shard_map/ppermute | solution.py:285
  9.8 27.6 %collective-permute-start.6 = (bf16[2,256]{1,0:T(2,128)(2,1)}, bf16[2,256]{1,0:T(2,128)(2,1)}, u32[]{:S(2)}, u32[]{:S(2)}) collective-permute-start(bf16[2,256]{1,0:T(2,128)(2,1)} %pad_maximum_fusion.18), channel_id=1, source_target_pairs={{0,1},{1,0},{2,3},{3,2},{4,5},{5,4},{6,7},{7,6},{8,9},{9,8},{10,11... | collective-permute-start | bytes 3080 | tf_op jit(solution)/shard_map/ppermute | solution.py:432
  14.3 47.6 %collective-permute-start.13 = (bf16[64,640]{1,0:T(8,128)(2,1)}, bf16[64,640]{1,0:T(8,128)(2,1)}, u32[]{:S(2)}, u32[]{:S(2)}) collective-permute-start(bf16[64,640]{1,0:T(8,128)(2,1)} %get-tuple-element.161), channel_id=1, source_target_pairs={{0,6},{1,7},{8,14},{9,15},{16,22},{17,23},{24,30},{25,31}} | collective-permute-start | bytes 245768 | tf_op jit(solution)/shard_map/ppermute | solution.py:285
  20.7 43.6 %collective-permute-start.14 = (bf16[64,640]{1,0:T(8,128)(2,1)}, bf16[64,640]{1,0:T(8,128)(2,1)S(1)}, u32[]{:S(2)}, u32[]{:S(2)}) collective-permute-start(bf16[64,640]{1,0:T(8,128)(2,1)} %get-tuple-element.160), channel_id=1, source_target_pairs={{0,4},{1,5},{2,6},{3,7},{8,12},{9,13},{10,14},{11,15},{16,20},{17,... | collective-permute-start | bytes 245768 | tf_op jit(solution)/shard_map/ppermute | solution.py:285
  61.9 33.6 %collective-permute-start.23 = (bf16[64,2048]{1,0:T(8,128)(2,1)S(1)}, bf16[64,2048]{1,0:T(8,128)(2,1)S(1)}, u32[]{:S(2)}, u32[]{:S(2)}) collective-permute-start(bf16[64,2048]{1,0:T(8,128)(2,1)S(1)} %dynamic-slice_convert_fusion.3), channel_id=1, source_target_pairs={{0,16},{1,17},{2,18},{3,19},{4,20},{5,21},{6,22},{7,23},{8,9},{9,8... | collective-permute-start | bytes 786440 | tf_op jit(solution)/shard_map/ppermute | solution.py:324
  64.3 115.4 %collective-permute-start.47 = (bf16[176,2048]{1,0:T(8,128)(2,1)}, bf16[176,2048]{1,0:T(8,128)(2,1)}, u32[]{:S(2)}, u32[]{:S(2)}) collective-permute-start(bf16[176,2048]{1,0:T(8,128)(2,1)} %dynamic-slice_convert_fusion), channel_id=1, source_target_pairs={{0,16},{1,17},{2,18},{3,19},{4,20},{5,21},{6,22},{7,23},{8,9},{9,8... | collective-permute-start | bytes 2162696 | tf_op jit(solution)/shard_map/ppermute | solution.py:324
  114.7 18.1 %collective-permute-start.25 = (bf16[4,64,2048]{2,1,0:T(8,128)(2,1)S(1)}, bf16[4,64,2048]{2,1,0:T(8,128)(2,1)S(1)}, u32[]{:S(2)}, u32[]{:S(2)}) collective-permute-start(bf16[4,64,2048]{2,1,0:T(8,128)(2,1)S(1)} %pad_maximum_fusion.9), channel_id=1, source_target_pairs={{0,8},{8,0},{16,24},{24,16},{1,9},{9,1},{17,25},{25,17},{2,10},{10... | collective-permute-start | bytes 3145736 | tf_op jit(solution)/shard_map/ppermute | solution.py:328
  180.9 35.5 %collective-permute-start.48 = (bf16[2,176,2048]{2,1,0:T(8,128)(2,1)S(1)}, bf16[2,176,2048]{2,1,0:T(8,128)(2,1)S(1)}, u32[]{:S(2)}, u32[]{:S(2)}) collective-permute-start(bf16[2,176,2048]{2,1,0:T(8,128)(2,1)S(1)} %pad_maximum_fusion.7), channel_id=1, source_target_pairs={{0,1},{1,0},{2,3},{3,2},{4,5},{5,4},{6,7},{7,6},{8,24},{9,25},{10,... | collective-permute-start | bytes 4325384 | tf_op jit(solution)/shard_map/ppermute | solution.py:326
  182.5 16.7 %collective-permute-start.29 = (bf16[128,2048]{1,0:T(8,128)(2,1)}, bf16[128,2048]{1,0:T(8,128)(2,1)S(1)}, u32[]{:S(2)}, u32[]{:S(2)}) collective-permute-start(bf16[128,2048]{1,0:T(8,128)(2,1)} %get-tuple-element.116), channel_id=1, source_target_pairs={{6,4},{7,5},{14,12},{15,13},{22,20},{23,21},{30,28},{31,29}} | collective-permute-start | bytes 1572872 | tf_op jit(solution)/shard_map/ppermute | solution.py:285
  197.9 17.3 %collective-permute-start.39 = (bf16[64,2816]{1,0:T(8,128)(2,1)S(1)}, bf16[64,2816]{1,0:T(8,128)(2,1)S(1)}, u32[]{:S(2)}, u32[]{:S(2)}) collective-permute-start(bf16[64,2816]{1,0:T(8,128)(2,1)S(1)} %bitcast.678), channel_id=1, source_target_pairs={{0,4},{1,5},{2,6},{3,7},{8,12},{9,13},{10,14},{11,15},{16,20},{17,... | collective-permute-start | bytes 1081352 | tf_op jit(solution)/shard_map/ppermute | solution.py:285
  199.2 21.5 %collective-permute-start.40 = (bf16[64,2816]{1,0:T(8,128)(2,1)S(1)}, bf16[64,2816]{1,0:T(8,128)(2,1)S(1)}, u32[]{:S(2)}, u32[]{:S(2)}) collective-permute-start(bf16[64,2816]{1,0:T(8,128)(2,1)S(1)} %bitcast.674), channel_id=1, source_target_pairs={{0,2},{1,3},{2,4},{3,5},{4,6},{5,7},{8,10},{9,11},{10,12},{11,13},... | collective-permute-start | bytes 1081352 | tf_op jit(solution)/shard_map/ppermute | solution.py:285
  201.9 65.4 %collective-permute-start.30 = (bf16[128,2048]{1,0:T(8,128)(2,1)}, bf16[128,2048]{1,0:T(8,128)(2,1)}, u32[]{:S(2)}, u32[]{:S(2)}) collective-permute-start(bf16[128,2048]{1,0:T(8,128)(2,1)} %get-tuple-element.114), channel_id=1, source_target_pairs={{4,2},{5,3},{6,4},{7,5},{12,10},{13,11},{14,12},{15,13},{20,18},{2... | collective-permute-start | bytes 1572872 | tf_op jit(solution)/shard_map/ppermute | solution.py:285
  215.1 33.3 %collective-permute-start.42 = (bf16[64,2816]{1,0:T(8,128)(2,1)S(1)}, bf16[64,2816]{1,0:T(8,128)(2,1)S(1)}, u32[]{:S(2)}, u32[]{:S(2)}) collective-permute-start(bf16[64,2816]{1,0:T(8,128)(2,1)S(1)} %bitcast.676), channel_id=1, source_target_pairs={{4,0},{5,1},{6,2},{7,3},{12,8},{13,9},{14,10},{15,11},{20,16},{21,... | collective-permute-start | bytes 1081352 | tf_op jit(solution)/shard_map/ppermute | solution.py:285
  216.4 33.4 %collective-permute-start.43 = (bf16[64,2816]{1,0:T(8,128)(2,1)S(1)}, bf16[64,2816]{1,0:T(8,128)(2,1)S(1)}, u32[]{:S(2)}, u32[]{:S(2)}) collective-permute-start(bf16[64,2816]{1,0:T(8,128)(2,1)S(1)} %bitcast.675), channel_id=1, source_target_pairs={{6,0},{7,1},{14,8},{15,9},{22,16},{23,17},{30,24},{31,25}} | collective-permute-start | bytes 1081352 | tf_op jit(solution)/shard_map/ppermute | solution.py:285
  220.7 88.2 %collective-permute-start.49 = (bf16[4,176,2048]{2,1,0:T(8,128)(2,1)}, bf16[4,176,2048]{2,1,0:T(8,128)(2,1)}, u32[]{:S(2)}, u32[]{:S(2)}) collective-permute-start(bf16[4,176,2048]{2,1,0:T(8,128)(2,1)} %pad_maximum_fusion.2), channel_id=1, source_target_pairs={{0,8},{8,0},{16,24},{24,16},{1,9},{9,1},{17,25},{25,17},{2,10},{10... | collective-permute-start | bytes 8650760 | tf_op jit(solution)/shard_map/ppermute | solution.py:328
  272.5 26.4 %collective-permute-start.44 = (bf16[4,64,2816]{2,0,1:T(4,128)(2,1)S(1)}, bf16[4,64,2816]{2,0,1:T(4,128)(2,1)S(1)}, u32[]{:S(2)}, u32[]{:S(2)}) collective-permute-start(bf16[4,64,2816]{2,0,1:T(4,128)(2,1)S(1)} %constant_dynamic-slice_fusion.6), channel_id=1, source_target_pairs={{0,16},{1,17},{2,18},{3,19},{4,20},{5,21},{6,22},{7,23},{8,9},{9,8... | collective-permute-start | bytes 4325384 | tf_op jit(solution)/shard_map/ppermute | solution.py:324
  281.4 32.0 %collective-permute-start.50 = (bf16[128,2048]{1,0:T(8,128)(2,1)S(1)}, bf16[128,2048]{1,0:T(8,128)(2,1)S(1)}, u32[]{:S(2)}, u32[]{:S(2)}) collective-permute-start(bf16[128,2048]{1,0:T(8,128)(2,1)S(1)} %bitcast.649), channel_id=1, source_target_pairs={{0,2},{1,3},{2,4},{3,5},{4,6},{5,7},{8,10},{9,11},{10,12},{11,13},... | collective-permute-start | bytes 1572872 | tf_op jit(solution)/shard_map/ppermute | solution.py:285
  300.9 56.6 %collective-permute-start.45 = (bf16[2,4,64,2816]{3,1,2,0:T(4,128)(2,1)S(1)}, bf16[2,4,64,2816]{3,1,2,0:T(4,128)(2,1)S(1)}, u32[]{:S(2)}, u32[]{:S(2)}) collective-permute-start(bf16[2,4,64,2816]{3,1,2,0:T(4,128)(2,1)S(1)} %pad_maximum_fusion.1), channel_id=1, source_target_pairs={{0,1},{1,0},{2,3},{3,2},{4,5},{5,4},{6,7},{7,6},{8,24},{9,25},{10,... | collective-permute-start | bytes 8650760 | tf_op jit(solution)/shard_map/ppermute | solution.py:326
  302.7 20.6 %collective-permute-start.32 = (bf16[128,2048]{1,0:T(8,128)(2,1)S(1)}, bf16[128,2048]{1,0:T(8,128)(2,1)S(1)}, u32[]{:S(2)}, u32[]{:S(2)}) collective-permute-start(bf16[128,2048]{1,0:T(8,128)(2,1)S(1)} %multiply_convert_fusion.3), channel_id=1, source_target_pairs={{0,2},{1,3},{2,4},{3,5},{4,6},{5,7},{8,10},{9,11},{10,12},{11,13},... | collective-permute-start | bytes 1572872 | tf_op jit(solution)/shard_map/ppermute | solution.py:285
  307.6 19.7 %collective-permute-start.35 = (bf16[128,2048]{1,0:T(8,128)(2,1)S(1)}, bf16[128,2048]{1,0:T(8,128)(2,1)S(1)}, u32[]{:S(2)}, u32[]{:S(2)}) collective-permute-start(bf16[128,2048]{1,0:T(8,128)(2,1)S(1)} %multiply_convert_fusion.3), channel_id=1, source_target_pairs={{2,0},{3,1},{4,2},{5,3},{6,4},{7,5},{10,8},{11,9},{12,10},{13,11},... | collective-permute-start | bytes 1572872 | tf_op jit(solution)/shard_map/ppermute | solution.py:285
  308.9 26.7 %collective-permute-start.53 = (bf16[128,2048]{1,0:T(8,128)(2,1)S(1)}, bf16[128,2048]{1,0:T(8,128)(2,1)S(1)}, u32[]{:S(2)}, u32[]{:S(2)}) collective-permute-start(bf16[128,2048]{1,0:T(8,128)(2,1)S(1)} %bitcast.650), channel_id=1, source_target_pairs={{2,0},{3,1},{4,2},{5,3},{6,4},{7,5},{10,8},{11,9},{12,10},{13,11},... | collective-permute-start | bytes 1572872 | tf_op jit(solution)/shard_map/ppermute | solution.py:285
  313.4 23.5 %collective-permute-start.51 = (bf16[128,2048]{1,0:T(8,128)(2,1)S(1)}, bf16[128,2048]{1,0:T(8,128)(2,1)S(1)}, u32[]{:S(2)}, u32[]{:S(2)}) collective-permute-start(bf16[128,2048]{1,0:T(8,128)(2,1)S(1)} %collective-permute-done.50), channel_id=1, source_target_pairs={{0,2},{1,3},{2,4},{3,5},{4,6},{5,7},{8,10},{9,11},{10,12},{11,13},... | collective-permute-start | bytes 1572872 | tf_op jit(solution)/shard_map/ppermute | solution.py:285
  323.4 22.9 %collective-permute-start.33 = (bf16[128,2048]{1,0:T(8,128)(2,1)S(1)}, bf16[128,2048]{1,0:T(8,128)(2,1)S(1)}, u32[]{:S(2)}, u32[]{:S(2)}) collective-permute-start(bf16[128,2048]{1,0:T(8,128)(2,1)S(1)} %collective-permute-done.32), channel_id=1, source_target_pairs={{0,2},{1,3},{2,4},{3,5},{4,6},{5,7},{8,10},{9,11},{10,12},{11,13},... | collective-permute-start | bytes 1572872 | tf_op jit(solution)/shard_map/ppermute | solution.py:285
  327.3 22.7 %collective-permute-start.36 = (bf16[128,2048]{1,0:T(8,128)(2,1)S(1)}, bf16[128,2048]{1,0:T(8,128)(2,1)S(1)}, u32[]{:S(2)}, u32[]{:S(2)}) collective-permute-start(bf16[128,2048]{1,0:T(8,128)(2,1)S(1)} %collective-permute-done.35), channel_id=1, source_target_pairs={{2,0},{3,1},{4,2},{5,3},{6,4},{7,5},{10,8},{11,9},{12,10},{13,11},... | collective-permute-start | bytes 1572872 | tf_op jit(solution)/shard_map/ppermute | solution.py:285
  335.6 20.5 %collective-permute-start.54 = (bf16[128,2048]{1,0:T(8,128)(2,1)S(1)}, bf16[128,2048]{1,0:T(8,128)(2,1)S(1)}, u32[]{:S(2)}, u32[]{:S(2)}) collective-permute-start(bf16[128,2048]{1,0:T(8,128)(2,1)S(1)} %collective-permute-done.53), channel_id=1, source_target_pairs={{2,0},{3,1},{4,2},{5,3},{6,4},{7,5},{10,8},{11,9},{12,10},{13,11},... | collective-permute-start | bytes 1572872 | tf_op jit(solution)/shard_map/ppermute | solution.py:285
  336.9 20.5 %collective-permute-start.52 = (bf16[128,2048]{1,0:T(8,128)(2,1)S(1)}, bf16[128,2048]{1,0:T(8,128)(2,1)S(1)}, u32[]{:S(2)}, u32[]{:S(2)}) collective-permute-start(bf16[128,2048]{1,0:T(8,128)(2,1)S(1)} %collective-permute-done.51), channel_id=1, source_target_pairs={{0,2},{1,3},{2,4},{3,5},{4,6},{5,7},{8,10},{9,11},{10,12},{11,13},... | collective-permute-start | bytes 1572872 | tf_op jit(solution)/shard_map/ppermute | solution.py:285
  346.3 16.2 %collective-permute-start.34 = (bf16[128,2048]{1,0:T(8,128)(2,1)S(1)}, bf16[128,2048]{1,0:T(8,128)(2,1)S(1)}, u32[]{:S(2)}, u32[]{:S(2)}) collective-permute-start(bf16[128,2048]{1,0:T(8,128)(2,1)S(1)} %collective-permute-done.33), channel_id=1, source_target_pairs={{0,2},{1,3},{2,4},{3,5},{4,6},{5,7},{8,10},{9,11},{10,12},{11,13},... | collective-permute-start | bytes 1572872 | tf_op jit(solution)/shard_map/ppermute | solution.py:285
  444.7 22.2 %collective-permute-start.61 = (bf16[128,2048]{1,0:T(8,128)(2,1)S(1)}, bf16[128,2048]{1,0:T(8,128)(2,1)S(1)}, u32[]{:S(2)}, u32[]{:S(2)}) collective-permute-start(bf16[128,2048]{1,0:T(8,128)(2,1)S(1)} %fusion.26), channel_id=1, source_target_pairs={{2,0},{3,1},{4,2},{5,3},{6,4},{7,5},{10,8},{11,9},{12,10},{13,11},... | collective-permute-start | bytes 1572872 | tf_op jit(solution)/shard_map/ppermute | solution.py:285
  454.1 52.8 %collective-permute-start.117 = (bf16[4,176,2048]{2,1,0:T(8,128)(2,1)S(1)}, bf16[4,176,2048]{2,1,0:T(8,128)(2,1)}, u32[]{:S(2)}, u32[]{:S(2)}) collective-permute-start(bf16[4,176,2048]{2,1,0:T(8,128)(2,1)S(1)} %dynamic-slice_bitcast_fusion.1), channel_id=1, source_target_pairs={{0,8},{8,0},{16,24},{24,16},{1,9},{9,1},{17,25},{25,17},{2,10},{10... | collective-permute-start | bytes 8650760 | tf_op jit(solution)/shard_map/ppermute | solution.py:347
  467.9 18.1 %collective-permute-start.62 = (bf16[128,2048]{1,0:T(8,128)(2,1)S(1)}, bf16[128,2048]{1,0:T(8,128)(2,1)S(1)}, u32[]{:S(2)}, u32[]{:S(2)}) collective-permute-start(bf16[128,2048]{1,0:T(8,128)(2,1)S(1)} %get-tuple-element.85), channel_id=1, source_target_pairs={{0,2},{1,3},{2,4},{3,5},{4,6},{5,7},{8,10},{9,11},{10,12},{11,13},... | collective-permute-start | bytes 1572872 | tf_op jit(solution)/shard_map/ppermute | solution.py:285
  484.7 174.6 %collective-permute-start.106 = (bf16[4,4,64,2816]{3,2,1,0:T(8,128)(2,1)}, bf16[4,4,64,2816]{3,2,1,0:T(8,128)(2,1)}, u32[]{:S(2)}, u32[]{:S(2)}) collective-permute-start(bf16[4,4,64,2816]{3,2,1,0:T(8,128)(2,1)} %dynamic-slice_bitcast_fusion), channel_id=1, source_target_pairs={{0,8},{8,0},{16,24},{24,16},{1,9},{9,1},{17,25},{25,17},{2,10},{10... | collective-permute-start | bytes 17301512 | tf_op jit(solution)/shard_map/ppermute | solution.py:347
  484.7 16.2 %collective-permute-start.65 = (bf16[128,2048]{1,0:T(8,128)(2,1)S(1)}, bf16[128,2048]{1,0:T(8,128)(2,1)S(1)}, u32[]{:S(2)}, u32[]{:S(2)}) collective-permute-start(bf16[128,2048]{1,0:T(8,128)(2,1)S(1)} %get-tuple-element.85), channel_id=1, source_target_pairs={{2,0},{3,1},{4,2},{5,3},{6,4},{7,5},{10,8},{11,9},{12,10},{13,11},... | collective-permute-start | bytes 1572872 | tf_op jit(solution)/shard_map/ppermute | solution.py:285
  486.0 16.2 %collective-permute-start.63 = (bf16[128,2048]{1,0:T(8,128)(2,1)S(1)}, bf16[128,2048]{1,0:T(8,128)(2,1)S(1)}, u32[]{:S(2)}, u32[]{:S(2)}) collective-permute-start(bf16[128,2048]{1,0:T(8,128)(2,1)S(1)} %collective-permute-done.62), channel_id=1, source_target_pairs={{0,2},{1,3},{2,4},{3,5},{4,6},{5,7},{8,10},{9,11},{10,12},{11,13},... | collective-permute-start | bytes 1572872 | tf_op jit(solution)/shard_map/ppermute | solution.py:285
  558.6 48.3 %collective-permute-start.118 = (bf16[2,176,2048]{2,1,0:T(8,128)(2,1)}, bf16[2,176,2048]{2,1,0:T(8,128)(2,1)}, u32[]{:S(2)}, u32[]{:S(2)}) collective-permute-start(bf16[2,176,2048]{2,1,0:T(8,128)(2,1)} %bitcast_select_fusion.2), channel_id=1, source_target_pairs={{0,1},{1,0},{2,3},{3,2},{4,5},{5,4},{6,7},{7,6},{8,24},{9,25},{10,... | collective-permute-start | bytes 4325384 | tf_op jit(solution)/shard_map/ppermute | solution.py:356
  566.0 36.4 %collective-permute-start.68 = (bf16[128,2048]{1,0:T(8,128)(2,1)}, bf16[128,2048]{1,0:T(8,128)(2,1)}, u32[]{:S(2)}, u32[]{:S(2)}) collective-permute-start(bf16[128,2048]{1,0:T(8,128)(2,1)} %get-tuple-element.107), channel_id=1, source_target_pairs={{0,2},{1,3},{8,10},{9,11},{16,18},{17,19},{24,26},{25,27}} | collective-permute-start | bytes 1572872 | tf_op jit(solution)/shard_map/ppermute | solution.py:285
  598.5 25.4 %collective-permute-start.71 = (bf16[128,2048]{1,0:T(8,128)(2,1)}, bf16[128,2048]{1,0:T(8,128)(2,1)}, u32[]{:S(2)}, u32[]{:S(2)}) collective-permute-start(bf16[128,2048]{1,0:T(8,128)(2,1)} %get-tuple-element.108), channel_id=1, source_target_pairs={{6,4},{7,5},{14,12},{15,13},{22,20},{23,21},{30,28},{31,29}} | collective-permute-start | bytes 1572872 | tf_op jit(solution)/shard_map/ppermute | solution.py:285
  601.5 20.6 %collective-permute-start.101 = (bf16[4,64,2048]{2,1,0:T(8,128)(2,1)S(1)}, bf16[4,64,2048]{2,1,0:T(8,128)(2,1)}, u32[]{:S(2)}, u32[]{:S(2)}) collective-permute-start(bf16[4,64,2048]{2,1,0:T(8,128)(2,1)S(1)} %dynamic-slice_bitcast_fusion.7), channel_id=1, source_target_pairs={{0,8},{8,0},{16,24},{24,16},{1,9},{9,1},{17,25},{25,17},{2,10},{10... | collective-permute-start | bytes 3145736 | tf_op jit(solution)/shard_map/ppermute | solution.py:347
  606.9 33.8 %collective-permute-start.78 = (bf16[128,2048]{1,0:T(8,128)(2,1)}, bf16[128,2048]{1,0:T(8,128)(2,1)S(1)}, u32[]{:S(2)}, u32[]{:S(2)}) collective-permute-start(bf16[128,2048]{1,0:T(8,128)(2,1)} %get-tuple-element.104), channel_id=1, source_target_pairs={{6,4},{7,5},{14,12},{15,13},{22,20},{23,21},{30,28},{31,29}} | collective-permute-start | bytes 1572872 | tf_op jit(solution)/shard_map/ppermute | solution.py:285
  622.1 32.5 %collective-permute-start.90 = (bf16[4,4,64,640]{3,2,1,0:T(8,128)(2,1)S(1)}, bf16[4,4,64,640]{3,2,1,0:T(8,128)(2,1)S(1)}, u32[]{:S(2)}, u32[]{:S(2)}) collective-permute-start(bf16[4,4,64,640]{3,2,1,0:T(8,128)(2,1)S(1)} %copy-done.38), channel_id=1, source_target_pairs={{0,8},{8,0},{16,24},{24,16},{1,9},{9,1},{17,25},{25,17},{2,10},{10... | collective-permute-start | bytes 3932168 | tf_op jit(solution)/shard_map/ppermute | solution.py:347
  623.8 30.2 %collective-permute-start.119 = (bf16[176,2048]{1,0:T(8,128)(2,1)S(1)}, bf16[176,2048]{1,0:T(8,128)(2,1)S(1)}, u32[]{:S(2)}, u32[]{:S(2)}) collective-permute-start(bf16[176,2048]{1,0:T(8,128)(2,1)S(1)} %dynamic-slice_bitcast_fusion.8), channel_id=1, source_target_pairs={{0,16},{1,17},{2,18},{3,19},{4,20},{5,21},{6,22},{7,23},{8,9},{9,8... | collective-permute-start | bytes 2162696 | tf_op jit(solution)/shard_map/ppermute | solution.py:359
  640.7 30.5 %collective-permute-start.72 = (bf16[128,2048]{1,0:T(8,128)(2,1)}, bf16[128,2048]{1,0:T(8,128)(2,1)}, u32[]{:S(2)}, u32[]{:S(2)}) collective-permute-start(bf16[128,2048]{1,0:T(8,128)(2,1)} %get-tuple-element.106), channel_id=1, source_target_pairs={{4,2},{5,3},{6,4},{7,5},{12,10},{13,11},{14,12},{15,13},{20,18},{2... | collective-permute-start | bytes 1572872 | tf_op jit(solution)/shard_map/ppermute | solution.py:285
  647.5 51.0 %collective-permute-start.70 = (bf16[128,2048]{1,0:T(8,128)(2,1)}, bf16[128,2048]{1,0:T(8,128)(2,1)}, u32[]{:S(2)}, u32[]{:S(2)}) collective-permute-start(bf16[128,2048]{1,0:T(8,128)(2,1)} %get-tuple-element.105), channel_id=1, source_target_pairs={{0,2},{1,3},{2,4},{3,5},{4,6},{5,7},{8,10},{9,11},{10,12},{11,13},... | collective-permute-start | bytes 1572872 | tf_op jit(solution)/shard_map/ppermute | solution.py:285
  654.6 18.0 %collective-permute-start.79 = (bf16[128,2048]{1,0:T(8,128)(2,1)}, bf16[128,2048]{1,0:T(8,128)(2,1)}, u32[]{:S(2)}, u32[]{:S(2)}) collective-permute-start(bf16[128,2048]{1,0:T(8,128)(2,1)} %get-tuple-element.102), channel_id=1, source_target_pairs={{4,2},{5,3},{6,4},{7,5},{12,10},{13,11},{14,12},{15,13},{20,18},{2... | collective-permute-start | bytes 1572872 | tf_op jit(solution)/shard_map/ppermute | solution.py:285
  659.3 70.9 %collective-permute-start.77 = (bf16[128,2048]{1,0:T(8,128)(2,1)}, bf16[128,2048]{1,0:T(8,128)(2,1)}, u32[]{:S(2)}, u32[]{:S(2)}) collective-permute-start(bf16[128,2048]{1,0:T(8,128)(2,1)} %get-tuple-element.101), channel_id=1, source_target_pairs={{0,2},{1,3},{2,4},{3,5},{4,6},{5,7},{8,10},{9,11},{10,12},{11,13},... | collective-permute-start | bytes 1572872 | tf_op jit(solution)/shard_map/ppermute | solution.py:285
  668.1 41.3 %collective-permute-start.107 = (bf16[4,2,64,2816]{3,2,1,0:T(8,128)(2,1)S(1)}, bf16[4,2,64,2816]{3,2,1,0:T(8,128)(2,1)S(1)}, u32[]{:S(2)}, u32[]{:S(2)}) collective-permute-start(bf16[4,2,64,2816]{3,2,1,0:T(8,128)(2,1)S(1)} %bitcast_select_fusion), channel_id=1, source_target_pairs={{0,1},{1,0},{2,3},{3,2},{4,5},{5,4},{6,7},{7,6},{8,24},{9,25},{10,... | collective-permute-start | bytes 8650760 | tf_op jit(solution)/shard_map/ppermute | solution.py:356
  671.2 26.1 %collective-permute-start.120 = (bf16[176,2048]{1,0:T(8,128)(2,1)S(1)}, bf16[176,2048]{1,0:T(8,128)(2,1)S(1)}, u32[]{:S(2)}, u32[]{:S(2)}) collective-permute-start(bf16[176,2048]{1,0:T(8,128)(2,1)S(1)} %fusion.6), channel_id=1, source_target_pairs={{0,16},{8,24},{16,0},{24,8},{1,17},{9,25},{17,1},{25,9},{2,18},{10... | collective-permute-start | bytes 2162696 | tf_op jit(solution)/shard_map/ppermute | solution.py:363
  672.6 23.4 %collective-permute-start.103 = (bf16[64,2048]{1,0:T(8,128)(2,1)S(1)}, bf16[64,2048]{1,0:T(8,128)(2,1)S(1)}, u32[]{:S(2)}, u32[]{:S(2)}) collective-permute-start(bf16[64,2048]{1,0:T(8,128)(2,1)S(1)} %dynamic-slice_bitcast_fusion.24), channel_id=1, source_target_pairs={{0,16},{1,17},{2,18},{3,19},{4,20},{5,21},{6,22},{7,23},{8,9},{9,8... | collective-permute-start | bytes 786440 | tf_op jit(solution)/shard_map/ppermute | solution.py:359
  697.4 29.4 %collective-permute-start.91 = (bf16[4,2,64,640]{3,2,0,1:T(8,128)(2,1)S(1)}, bf16[4,2,64,640]{3,2,0,1:T(8,128)(2,1)S(1)}, u32[]{:S(2)}, u32[]{:S(2)}) collective-permute-start(bf16[4,2,64,640]{3,2,0,1:T(8,128)(2,1)S(1)} %copy-done.39), channel_id=1, source_target_pairs={{0,1},{1,0},{2,3},{3,2},{4,5},{5,4},{6,7},{7,6},{8,24},{9,25},{10,... | collective-permute-start | bytes 1966088 | tf_op jit(solution)/shard_map/ppermute | solution.py:356
  698.5 36.2 %collective-permute-start.80 = (bf16[128,2048]{1,0:T(8,128)(2,1)S(1)}, bf16[128,2048]{1,0:T(8,128)(2,1)S(1)}, u32[]{:S(2)}, u32[]{:S(2)}) collective-permute-start(bf16[128,2048]{1,0:T(8,128)(2,1)S(1)} %fusion.13), channel_id=1, source_target_pairs={{2,0},{3,1},{4,2},{5,3},{6,4},{7,5},{10,8},{11,9},{12,10},{13,11},... | collective-permute-start | bytes 1572872 | tf_op jit(solution)/shard_map/ppermute | solution.py:285
  707.0 21.8 %collective-permute-start.104 = (bf16[64,2048]{1,0:T(8,128)(2,1)S(1)}, bf16[64,2048]{1,0:T(8,128)(2,1)S(1)}, u32[]{:S(2)}, u32[]{:S(2)}) collective-permute-start(bf16[64,2048]{1,0:T(8,128)(2,1)S(1)} %fusion.39), channel_id=1, source_target_pairs={{0,16},{8,24},{16,0},{24,8},{1,17},{9,25},{17,1},{25,9},{2,18},{10... | collective-permute-start | bytes 786440 | tf_op jit(solution)/shard_map/ppermute | solution.py:363
  709.3 168.2 %collective-permute-start.121 = (bf16[2,176,2048]{2,1,0:T(8,128)(2,1)S(1)}, bf16[2,176,2048]{2,1,0:T(8,128)(2,1)S(1)}, u32[]{:S(2)}, u32[]{:S(2)}) collective-permute-start(bf16[2,176,2048]{2,1,0:T(8,128)(2,1)S(1)} %maximum_select_fusion.5), channel_id=1, source_target_pairs={{0,8},{8,0},{16,24},{24,16},{1,9},{9,1},{17,25},{25,17},{2,10},{10... | collective-permute-start | bytes 4325384 | tf_op jit(solution)/shard_map/ppermute | solution.py:367
  726.8 28.6 %collective-permute-start.108 = (bf16[4,64,2816]{2,1,0:T(8,128)(2,1)S(1)}, bf16[4,64,2816]{2,1,0:T(8,128)(2,1)S(1)}, u32[]{:S(2)}, u32[]{:S(2)}) collective-permute-start(bf16[4,64,2816]{2,1,0:T(8,128)(2,1)S(1)} %dynamic-slice_bitcast_fusion.2), channel_id=1, source_target_pairs={{0,16},{1,17},{2,18},{3,19},{4,20},{5,21},{6,22},{7,23},{8,9},{9,8... | collective-permute-start | bytes 4325384 | tf_op jit(solution)/shard_map/ppermute | solution.py:359
  728.9 22.5 %collective-permute-start.92 = (bf16[4,64,640]{2,1,0:T(8,128)(2,1)S(1)}, bf16[4,64,640]{2,1,0:T(8,128)(2,1)S(1)}, u32[]{:S(2)}, u32[]{:S(2)}) collective-permute-start(bf16[4,64,640]{2,1,0:T(8,128)(2,1)S(1)} %dynamic-slice_bitcast_fusion.23), channel_id=1, source_target_pairs={{0,16},{1,17},{2,18},{3,19},{4,20},{5,21},{6,22},{7,23},{8,9},{9,8... | collective-permute-start | bytes 983048 | tf_op jit(solution)/shard_map/ppermute | solution.py:359
  730.2 122.4 %collective-permute-start.105 = (bf16[2,64,2048]{2,1,0:T(8,128)(2,1)S(1)}, bf16[2,64,2048]{2,1,0:T(8,128)(2,1)S(1)}, u32[]{:S(2)}, u32[]{:S(2)}) collective-permute-start(bf16[2,64,2048]{2,1,0:T(8,128)(2,1)S(1)} %maximum_select_fusion.11), channel_id=1, source_target_pairs={{0,8},{8,0},{16,24},{24,16},{1,9},{9,1},{17,25},{25,17},{2,10},{10... | collective-permute-start | bytes 1572872 | tf_op jit(solution)/shard_map/ppermute | solution.py:367
  757.1 41.5 %collective-permute-start.94 = (bf16[64,640]{1,0:T(8,128)(2,1)S(1)}, bf16[64,640]{1,0:T(8,128)(2,1)S(1)}, u32[]{:S(2)}, u32[]{:S(2)}) collective-permute-start(bf16[64,640]{1,0:T(8,128)(2,1)S(1)} %get-tuple-element.153), channel_id=1, source_target_pairs={{0,4},{1,5},{2,6},{3,7},{8,12},{9,13},{10,14},{11,15},{16,20},{17,... | collective-permute-start | bytes 245768 | tf_op jit(solution)/shard_map/ppermute | solution.py:285
  758.4 40.2 %collective-permute-start.95 = (bf16[64,640]{1,0:T(8,128)(2,1)S(1)}, bf16[64,640]{1,0:T(8,128)(2,1)S(1)}, u32[]{:S(2)}, u32[]{:S(2)}) collective-permute-start(bf16[64,640]{1,0:T(8,128)(2,1)S(1)} %get-tuple-element.152), channel_id=1, source_target_pairs={{0,2},{1,3},{2,4},{3,5},{4,6},{5,7},{8,10},{9,11},{10,12},{11,13},... | collective-permute-start | bytes 245768 | tf_op jit(solution)/shard_map/ppermute | solution.py:285
  776.3 20.6 %collective-permute-start.111 = (bf16[64,2816]{1,0:T(8,128)(2,1)S(1)}, bf16[64,2816]{1,0:T(8,128)(2,1)S(1)}, u32[]{:S(2)}, u32[]{:S(2)}) collective-permute-start(bf16[64,2816]{1,0:T(8,128)(2,1)S(1)} %get-tuple-element.121), channel_id=1, source_target_pairs={{0,2},{1,3},{2,4},{3,5},{4,6},{5,7},{8,10},{9,11},{10,12},{11,13},... | collective-permute-start | bytes 1081352 | tf_op jit(solution)/shard_map/ppermute | solution.py:285
  798.7 45.6 %collective-permute-start.96 = (bf16[64,640]{1,0:T(8,128)(2,1)S(1)}, bf16[64,640]{1,0:T(8,128)(2,1)S(1)}, u32[]{:S(2)}, u32[]{:S(2)}) collective-permute-start(bf16[64,640]{1,0:T(8,128)(2,1)S(1)} %get-tuple-element.150), channel_id=1, source_target_pairs={{2,0},{3,1},{4,2},{5,3},{6,4},{7,5},{10,8},{11,9},{12,10},{13,11},... | collective-permute-start | bytes 245768 | tf_op jit(solution)/shard_map/ppermute | solution.py:285
  800.0 36.4 %collective-permute-start.113 = (bf16[64,2816]{1,0:T(8,128)(2,1)S(1)}, bf16[64,2816]{1,0:T(8,128)(2,1)S(1)}, u32[]{:S(2)}, u32[]{:S(2)}) collective-permute-start(bf16[64,2816]{1,0:T(8,128)(2,1)S(1)} %get-tuple-element.118), channel_id=1, source_target_pairs={{4,0},{5,1},{6,2},{7,3},{12,8},{13,9},{14,10},{15,11},{20,16},{21,... | collective-permute-start | bytes 1081352 | tf_op jit(solution)/shard_map/ppermute | solution.py:285
  810.3 26.1 %collective-permute-start.114 = (bf16[64,2816]{1,0:T(8,128)(2,1)S(1)}, bf16[64,2816]{1,0:T(8,128)(2,1)S(1)}, u32[]{:S(2)}, u32[]{:S(2)}) collective-permute-start(bf16[64,2816]{1,0:T(8,128)(2,1)S(1)} %get-tuple-element.117), channel_id=1, source_target_pairs={{6,0},{7,1},{14,8},{15,9},{22,16},{23,17},{30,24},{31,25}} | collective-permute-start | bytes 1081352 | tf_op jit(solution)/shard_map/ppermute | solution.py:285
  837.9 35.1 %collective-permute-start.115 = (bf16[64,4,2816]{2,0,1:T(8,128)(2,1)S(1)}, bf16[64,4,2816]{2,0,1:T(8,128)(2,1)S(1)}, u32[]{:S(2)}, u32[]{:S(2)}) collective-permute-start(bf16[64,4,2816]{2,0,1:T(8,128)(2,1)S(1)} %get-tuple-element.100), channel_id=1, source_target_pairs={{0,16},{8,24},{16,0},{24,8},{1,17},{9,25},{17,1},{25,9},{2,18},{10... | collective-permute-start | bytes 4325384 | tf_op jit(solution)/shard_map/ppermute | solution.py:363
  852.5 24.2 %collective-permute-start.99 = (bf16[64,4,640]{2,0,1:T(8,128)(2,1)S(1)}, bf16[64,4,640]{2,0,1:T(8,128)(2,1)S(1)}, u32[]{:S(2)}, u32[]{:S(2)}) collective-permute-start(bf16[64,4,640]{2,0,1:T(8,128)(2,1)S(1)} %get-tuple-element.147), channel_id=1, source_target_pairs={{0,16},{8,24},{16,0},{24,8},{1,17},{9,25},{17,1},{25,9},{2,18},{10... | collective-permute-start | bytes 983048 | tf_op jit(solution)/shard_map/ppermute | solution.py:363
  875.1 16.3 %collective-permute-start.116 = (bf16[2,64,4,2816]{3,1,2,0:T(8,128)(2,1)}, bf16[2,64,4,2816]{3,1,2,0:T(8,128)(2,1)}, u32[]{:S(2)}, u32[]{:S(2)}) collective-permute-start(bf16[2,64,4,2816]{3,1,2,0:T(8,128)(2,1)} %maximum_select_fusion.2), channel_id=1, source_target_pairs={{0,8},{8,0},{16,24},{24,16},{1,9},{9,1},{17,25},{25,17},{2,10},{10... | collective-permute-start | bytes 8650760 | tf_op jit(solution)/shard_map/ppermute | solution.py:367
  (114 other events, 1227.3 us)
